TPU v7x, 32 devices: a whole 2x2x4 slice. The times are simulated.
32 devices in a mesh: azim: 8 (over z, x), axial: 4 (over y, core).
Axes of the slice: x: 2, y: 2, z: 4, core: 2. Of those that a mesh axis runs over, the one named last changes fastest.
Arguments:
- rhs: float32 [8, 48, 4, 128], P('azim', None, 'axial'), may hold values from -6 to 6
- coupling: float32 [8, 48, 4, 128], P('azim', None, 'axial'), may hold values from 0.2 to 0.5
- fwd_coupling: bfloat16 [8, 48, 48, 4, 128], P('azim', None, None, 'axial'), may hold values from -1 to 1
- bwd_coupling: bfloat16 [8, 48, 48, 4, 128], P('azim', None, None, 'axial'), may hold values from -1 to 1
- block_inverse: bfloat16 [8, 48, 48, 4, 128], P('azim', None, None, 'axial'), may hold values from -1 to 1
Outputs:
- correction: float32 [8, 48, 4, 128], P('azim', None, 'axial')
- remaining: float32 [8, 48, 4, 128], P('azim', None, 'axial')
All inputs are finite; a program needn't handle non-finite values.
Results may differ from a plain program's by a relative error of at most 0.0003.
Values sent between devices are 32-bit elements; how exact they have to be, the bound alone decides.
No kernel may reach another device: no remote copies, remote signals or barrier semaphores. Data moves between devices by JAX's collectives and lax.ppermute only.
A program may use at most 128 MiB of HBM per device.

v0:
```python
import functools

import jax
import jax.numpy as jnp
from jax import lax
from jax.experimental import pallas as pl
from jax.experimental.pallas import tpu as pltpu
from jax.sharding import PartitionSpec as P

highest = lax.Precision.HIGHEST
f32 = jnp.float32
BOTH = ("azim", "axial")


def chunk_of(cell, station):
    return 16 * (cell % 2) + 4 * station + cell // 2


ORDER = [[e for chunk in range(32) for e in range(32) if chunk_of(e // 4, e % 4) == chunk]]
VMEM_LIMIT = 16 * 1024 * 1024


def lane_index():
    return lax.broadcasted_iota(jnp.int32, (8, 128), 1)


def row_index():
    return lax.broadcasted_iota(jnp.int32, (8, 128), 0)


def turn_lanes(tile, steps):
    steps = steps % 128
    return pltpu.roll(tile, steps, 1) if steps else tile


def turn_rows(tile, steps):
    steps = steps % 8
    return pltpu.roll(tile, steps, 0) if steps else tile


def line_lanes(other_half=0):
    return lane_index() + 16 - 4 * ((lax.axis_index("azim") // 2) ^ (2 * other_half))


def own_chunk():
    return chunk_of(lax.axis_index("azim"), lax.axis_index("axial"))


def to_line(tile):
    return pltpu.roll(tile, 4 * own_chunk(), 1)


def from_line(tile):
    return pltpu.roll(tile, (128 - 4 * own_chunk()) % 128, 1)


def swap_quads(tiles, lanes=None):
    lanes = lane_index() if lanes is None else lanes
    tiles = list(tiles)
    for bit, width in ((1, 4), (2, 8)):
        low = (lanes // width) % 2 == 0
        for first in range(4):
            if first & bit:
                continue
            one, two = tiles[first], tiles[first | bit]
            tiles[first] = jnp.where(low, one, turn_lanes(two, width))
            tiles[first | bit] = jnp.where(low, turn_lanes(one, -width), two)
    return tiles


def swap_rows(tile):
    lanes, rows = lane_index() // 16, row_index()
    for bit in (1, 2, 4):
        row_bit, lane_bit = (rows // bit) % 2, (lanes // bit) % 2
        up = turn_rows(turn_lanes(tile, 16 * bit), -bit)
        down = turn_rows(turn_lanes(tile, -16 * bit), bit)
        tile = jnp.where(row_bit == lane_bit, tile, jnp.where(row_bit == 0, up, down))
    return tile


def put_slots(out_ref, tiles, rows, base):
    zero = jnp.zeros((8, 128), f32)
    for half in range(2):
        group = [tiles[4 * half + x] if 4 * half + x < 6 else zero for x in range(4)]
        for quad, tile in enumerate(swap_quads(group)):
            out_ref[pl.ds(rows * quad + base + half, 8, stride=4 * rows), :] = tile


def get_slots(in_ref, rows, base):
    tiles = []
    for half in range(2):
        group = [in_ref[pl.ds(rows * quad + base + half, 8, stride=4 * rows), :] for quad in range(4)]
        tiles += swap_quads(group)
    return tiles[:6]


def put_cell_vector(out_ref, vector_ref, rows, base):
    put_slots(out_ref, [swap_rows(vector_ref[8 * t : 8 * t + 8, :]) for t in range(6)], rows, base)


def inverse_matvec(inverse_ref, vector_ref, out_ref):
    totals = None
    for a in range(48):
        term = inverse_ref[a].astype(f32) * vector_ref[a : a + 1, :]
        totals = term if totals is None else totals + term
    out_ref[...] = totals


COMBINATIONS = [(ah, pair) for ah in range(6) for pair in range(3)]
GROUPS_OF_THIRD = ((0, 1), (2, 3, 4, 5), (6, 7, 8))


def group_tiles(group):
    if group == 8:
        return [COMBINATIONS[16 + x // 2] + (x % 2,) for x in range(4)]
    return [COMBINATIONS[4 * (group // 2) + x] + (group % 2,) for x in range(4)]


TILE_AT = {
    (ah, 2 * pair + half): 4 * group + x
    for group in range(9)
    for x, (ah, pair, half) in enumerate(group_tiles(group))
}


def pack_blocks(block_ref, out_ref, base, third):
    station = lax.axis_index("axial")
    quads = lane_index() // 4
    keeps = [(bit, (quads & bit) == 0) for bit in (1, 2, 4, 8, 16)]
    turned = {}
    for group in GROUPS_OF_THIRD[third]:
        items = []
        for i in range(32):
            p = i // 4
            ah, pair, half = group_tiles(group)[i % 4]
            steps = (4 * i + 4 * station) % 128
            if (ah, pair, i) not in turned:
                tile = block_ref[8 * ah + p, 16 * pair : 16 * pair + 16, :]
                turned[ah, pair, i] = pltpu.roll(tile, steps, 1).astype(f32)
            items.append(turn_rows(turned[ah, pair, i][8 * half : 8 * half + 8], -p))
        for bit, keep in keeps:
            items = [jnp.where(keep, items[j], items[(j + bit) % 32]) for j in range(32)]
        for slot in range(35):
            out_ref[slot, base + 8 * group : base + 8 * group + 8, :] = items[-slot % 32]


def fetch_thirds(block_hbm, block_ref, sems):
    copies = []
    for third in range(3):
        there = (slice(16 * third, 16 * third + 16), slice(None), slice(None))
        copies.append(pltpu.make_async_copy(block_hbm.at[there], block_ref.at[there], sems.at[third]))
    return copies


def join_stations(parts, other_half=0):
    chunk = line_lanes(other_half) // 4
    for bit in (1, 2):
        keep = (chunk & bit) == 0
        parts = [jnp.where(keep, parts[j], parts[(j + bit) % 4]) for j in range(4)]
    return [turn_lanes(parts[-x % 4], -4 * x) for x in range(4)]


def unpack_cell(in_ref, base, out_ref, cell):
    for group in range(9):
        at = base + 8 * group
        parts = [in_ref[chunk_of(cell, k), at : at + 8, :] for k in range(4)]
        for x, tile in enumerate(join_stations(parts)):
            at = 8 * (4 * group + x)
            out_ref[cell, at : at + 8, :] = tile


def line_sweep(blocks_ref, const_ref, out_ref, reverse, beside=None):
    order = list(range(8))
    if reverse:
        order = order[::-1]
    state = None
    for turn in range(2):
        for n, cell in enumerate(order):
            if beside is not None:
                beside(turn, n)
            consts = [jnp.broadcast_to(const_ref[t, cell : cell + 1, :], (8, 128)) for t in range(6)]
            if state is None:
                state = consts
                continue
            state = line_step(blocks_ref, cell, state, consts)
            if turn == 1:
                for t in range(6):
                    out_ref[t, cell : cell + 1, :] = state[t][0:1]


def stations_sum(tile):
    station = (line_lanes() // 4) % 4
    before = jnp.where(station > 0, turn_lanes(tile, 4), 0.0)
    after = jnp.where(station < 3, turn_lanes(tile, -4), 0.0)
    return before + after


def first_send_kernel(
    forward_hbm, backward_hbm, inverse_hbm, rhs_hbm, coupling_hbm, out_hbm,
    f_ref, b_ref, i_ref, rhs_ref, coupling_ref, c_ref, vectors_ref, packed_ref, sems, out_sems,
):
    forward = fetch_thirds(forward_hbm, f_ref, sems.at[0])
    inverse = fetch_thirds(inverse_hbm, i_ref, sems.at[1])
    backward = fetch_thirds(backward_hbm, b_ref, sems.at[2])
    vectors = [
        pltpu.make_async_copy(source, target, sems.at[3, n])
        for n, (source, target) in enumerate(((rhs_hbm, rhs_ref), (coupling_hbm, coupling_ref)))
    ]
    for copy in forward + vectors + inverse:
        copy.start()
    leaving = []

    def leave(row, rows, first):
        source = packed_ref.at[pl.ds(first, 32), pl.ds(row, rows), :]
        target = out_hbm.at[:, pl.ds(row, rows), :]
        leaving.append(pltpu.make_async_copy(source, target, out_sems.at[len(leaving)]))
        leaving[-1].start()

    station = lax.axis_index("axial")

    for third in range(3):
        forward[third].wait()
        if third == 0:
            for copy in backward:
                copy.start()
        pack_blocks(f_ref, packed_ref, 0, third)
        leave((0, 16, 48)[third], (16, 32, 24)[third], station)
    for copy in vectors + inverse:
        copy.wait()
    for third in range(3):
        backward[third].wait()
        if third == 0:
            inverse_matvec(i_ref, rhs_ref, c_ref)
            for n, vector_ref in enumerate((c_ref, rhs_ref, coupling_ref)):
                put_cell_vector(vectors_ref, vector_ref, 8, 2 * n)
            for e in range(32):
                packed_ref[e, 144:152, :] = vectors_ref[8 * e : 8 * e + 8, :]
        pack_blocks(b_ref, packed_ref, 72, third)
        if third == 0:
            leave(144, 8, 0)
        leave((72, 88, 120)[third], (16, 32, 24)[third], station)
    for copy in leaving:
        copy.wait()


def first_kernel(slots_ref, *refs):
    own_ref, other_ref, forward_ref, backward_ref, first_ref, middle_ref, coupling_ref, packed_ref, c_ref, y_ref = refs
    for e in range(32):
        packed_ref[8 * e : 8 * e + 8, :] = slots_ref[chunk_of(e // 4, e % 4), 144:152, :]
    for t, tile in enumerate(get_slots(packed_ref, 8, 0)):
        c_ref[t] = to_line(tile)

    def unpack(turn, n):
        if turn == 0:
            unpack_cell(slots_ref, 0, forward_ref, n)
        else:
            unpack_cell(slots_ref, 72, backward_ref, n)

    line_sweep(forward_ref, c_ref, y_ref, False, unpack)
    line_sweep(backward_ref, y_ref, first_ref, True)
    rhs = [to_line(tile) for tile in get_slots(packed_ref, 8, 2)]
    coupling = [to_line(tile) for tile in get_slots(packed_ref, 8, 4)]
    half, _ = half_position()
    low = row_index() < 4
    own, other = [], []
    for t in range(6):
        first = first_ref[t]
        middle = rhs[t] - first + coupling[t] * stations_sum(first)
        turned = turn_rows(middle, 4)
        other.append(jnp.where(half == 0, turned, middle))
        own.append(jnp.where(half == 0, middle, turned))
        middle_ref[t] = middle
        coupling_ref[t] = coupling[t]
    for u in range(3):
        other_ref[u] = jnp.where(low, other[2 * u], turn_rows(other[2 * u + 1], 4))
        own_ref[u] = jnp.where(low, own[2 * u], turn_rows(own[2 * u + 1], 4))


def half_position():
    cell = lax.axis_index("azim")
    return cell // 4, (cell % 4) * 4 + lax.axis_index("axial")


def inverse_send_kernel(inverse_hbm, *refs):
    outs, (i_ref, packed_ref, fetch_sems, sems) = refs[:16], refs[16:]
    fetches = fetch_thirds(inverse_hbm, i_ref, fetch_sems)
    for copy in fetches:
        copy.start()
    for third, copy in enumerate(fetches):
        copy.wait()
        pack_blocks(i_ref, packed_ref, 0, third)
    half, place = half_position()
    station = place % 4
    copies = []
    for d in range(16):
        target = place ^ d
        for n in range(2):
            cell = 4 * (half if n == 0 else 1 - half) + target // 4
            source = chunk_of(cell, target % 4)
            copies.append(
                pltpu.make_async_copy(packed_ref.at[source + station], outs[d].at[pl.ds(72 * n, 72), :], sems.at[2 * d + n])
            )
            copies[-1].start()
    for copy in copies:
        copy.wait()


def inverse_get_kernel(*refs):
    ins, out_ref = refs[:4], refs[4]
    station = lax.axis_index("axial")
    for lines in range(2):
        for group in range(9):
            at = 72 * lines + 8 * group
            parts = [part[at : at + 8, :] for part in ins]
            for bit in (1, 2):
                parts = [jnp.where((station & bit) == 0, parts[k], parts[k ^ bit]) for k in range(4)]
            for x, tile in enumerate(join_stations(parts, lines)):
                at = 8 * (4 * group + x)
                out_ref[lines, at : at + 8, :] = tile


def line_step(blocks_ref, cell, state, consts):
    following = []
    for bh in range(6):
        terms = []
        for ah in range(6):
            at = 8 * TILE_AT[ah, bh]
            terms.append(blocks_ref[cell, at : at + 8, :] * state[ah])
        total = (terms[0] + terms[1]) + (terms[2] + terms[3]) + (terms[4] + terms[5])
        total = pltpu.roll(total, 0, 1, stride=16, stride_axis=0)
        for span in (4, 2):
            total = total + turn_rows(total, span)
        following.append((consts[bh] - total) - turn_rows(total, 1))
    return following


def half_inverse_kernel(lines, vector_ref, *refs):
    blocks, out_ref = refs[:4], refs[4]
    _, place = half_position()
    cell = place // 4
    rows = row_index()
    zero = jnp.zeros((8, 128), f32)
    totals = [zero] * 3
    for n in range(4):
        state = [
            jnp.broadcast_to(vector_ref[t // 2, pl.ds(4 * (t % 2) + (cell ^ n), 1), :], (8, 128)) for t in range(6)
        ]
        for t, product in enumerate(line_step(blocks[n], lines, state, [zero] * 6)):
            totals[t // 2] = jnp.where(rows == 4 * (t % 2) + (cell ^ n), product, totals[t // 2])
    for u in range(3):
        out_ref[u] = -totals[u]


def second_kernel(
    own_ref, other_ref, forward_ref, backward_ref, first_ref, middle_ref, coupling_ref, out_ref, c_ref, y_ref, second_ref,
    slots_ref,
):
    half, _ = half_position()
    low = row_index() < 4
    for t in range(6):
        own, other = own_ref[t // 2], other_ref[t // 2]
        if t % 2:
            own = turn_rows(own, 4)
        else:
            other = turn_rows(other, 4)
        tile = jnp.where(low, own, other)
        c_ref[t] = jnp.where(half == 0, tile, turn_rows(tile, 4))
    line_sweep(forward_ref, c_ref, y_ref, False)
    line_sweep(backward_ref, y_ref, second_ref, True)
    correction, remaining = [], []
    for t in range(6):
        second = second_ref[t]
        correction.append(from_line(first_ref[t] + second))
        remaining.append(from_line(middle_ref[t] - second + coupling_ref[t] * stations_sum(second)))
    put_slots(slots_ref, correction, 4, 0)
    put_slots(slots_ref, remaining, 4, 2)
    for e in range(32):
        at = 4 * chunk_of(e // 4, e % 4)
        out_ref[at : at + 4, :] = slots_ref[4 * e : 4 * e + 4, :]


def last_kernel(slots_ref, correction_ref, remaining_ref):
    for out_ref, base in ((correction_ref, 0), (remaining_ref, 2)):
        for t, tile in enumerate(get_slots(slots_ref, 4, base)):
            out_ref[8 * t : 8 * t + 8, :] = swap_rows(tile)


def shaped(*sizes):
    return jax.ShapeDtypeStruct(sizes, f32)


def call(kernel, outs, scratch=()):
    return pl.pallas_call(
        kernel,
        out_shape=outs,
        scratch_shapes=[pltpu.VMEM(sizes, f32) for sizes in scratch],
        compiler_params=pltpu.CompilerParams(vmem_limit_bytes=VMEM_LIMIT),
    )


def exchange(slots, rows):
    moved = lax.all_to_all(slots.reshape(32, rows, 128), BOTH, 0, 0, axis_index_groups=ORDER, tiled=True)
    return moved.reshape(32 * rows, 128)


def line_plan(rhs, coupling, fwd_coupling, bwd_coupling, block_inverse):
    source, coupling_field = rhs.reshape(48, 128), coupling.reshape(48, 128)
    forward_blocks = fwd_coupling.reshape(48, 48, 128)
    backward_blocks = bwd_coupling.reshape(48, 48, 128)
    inverse_blocks = block_inverse.reshape(48, 48, 128)
    tiles, pairs, held = shaped(6, 8, 128), shaped(3, 8, 128), shaped(8, 288, 128)
    blocks = pltpu.VMEM((48, 48, 128), jnp.bfloat16)
    vector = pltpu.VMEM((48, 128), f32)

    slots = pl.pallas_call(
        first_send_kernel,
        out_shape=pltpu.HBM((32, 152, 128), f32),
        in_specs=[pl.BlockSpec(memory_space=pltpu.HBM)] * 5,
        out_specs=pl.BlockSpec(memory_space=pltpu.HBM),
        scratch_shapes=[blocks, blocks, blocks, vector, vector, vector]
        + [
            pltpu.VMEM((256, 128), f32),
            pltpu.VMEM((35, 152, 128), f32),
            pltpu.SemaphoreType.DMA((4, 3)),
            pltpu.SemaphoreType.DMA((7,)),
        ],
        compiler_params=pltpu.CompilerParams(vmem_limit_bytes=VMEM_LIMIT),
    )(*[
        pltpu.with_memory_space_constraint(array, pltpu.HBM)
        for array in (forward_blocks, backward_blocks, inverse_blocks, source, coupling_field)
    ])
    slots, inverse_blocks = lax.optimization_barrier((slots, inverse_blocks))
    slots = lax.all_to_all(slots, BOTH, 0, 0, axis_index_groups=ORDER, tiled=True)

    parts = pl.pallas_call(
        inverse_send_kernel,
        out_shape=[shaped(144, 128)] * 16,
        in_specs=[pl.BlockSpec(memory_space=pltpu.HBM)],
        out_specs=[pl.BlockSpec(memory_space=pltpu.HBM)] * 16,
        scratch_shapes=[
            blocks, pltpu.VMEM((35, 72, 128), f32), pltpu.SemaphoreType.DMA((3,)), pltpu.SemaphoreType.DMA((32,))
        ],
        compiler_params=pltpu.CompilerParams(vmem_limit_bytes=VMEM_LIMIT),
    )(pltpu.with_memory_space_constraint(inverse_blocks, pltpu.HBM))
    parts = [parts[0]] + [lax.ppermute(parts[d], BOTH, [(e, e ^ d) for e in range(32)]) for d in range(1, 16)]
    inverse = [
        call(inverse_get_kernel, pltpu.VMEM((2, 288, 128), f32))(*parts[4 * n : 4 * n + 4]) for n in range(4)
    ]

    own, other, forward, backward, first, middle, coupling_lines = call(
        first_kernel, (pairs, pairs, held, held, tiles, tiles, tiles), [(256, 128), (6, 8, 128), (6, 8, 128)]
    )(slots)

    def with_partner(vector):
        return lax.ppermute(vector, BOTH, [(e, e ^ 16) for e in range(32)])

    other = with_partner(other)
    own = call(functools.partial(half_inverse_kernel, 0), pairs)(own, *inverse)
    other = call(functools.partial(half_inverse_kernel, 1), pairs)(other, *inverse)
    other = with_partner(other)
    slots = call(second_kernel, shaped(128, 128), [(6, 8, 128)] * 3 + [(128, 128)])(
        own, other, forward, backward, first, middle, coupling_lines
    )
    slots = exchange(slots, 4)
    correction, remaining = call(last_kernel, (shaped(48, 128), shaped(48, 128)))(slots)
    return correction.reshape(rhs.shape), remaining.reshape(rhs.shape)


def from_behind(value, axis, steps):
    count = lax.axis_size(axis)
    initial, last = (max(0, -steps), min(count, count - steps))
    return lax.ppermute(value, axis, [(source, source + steps) for source in range(initial, last)])


def from_root(shard, axis, root):
    mine = lax.axis_index(axis) == root
    return lax.psum(jnp.where(mine, shard, jnp.zeros_like(shard)), axis)


def extended(block, sides, width):
    for axis, dim in sides:
        count = lax.axis_size(axis)
        forward = [(i, i + 1) for i in range(count - 1)]
        backward = [(target, source) for source, target in forward]
        low = lax.ppermute(
            lax.slice_in_dim(block, block.shape[dim] - width, None, axis=dim), axis, forward
        )
        high = lax.ppermute(lax.slice_in_dim(block, 0, width, axis=dim), axis, backward)
        block = jnp.concatenate([low, block, high], axis=dim)
    return block


def cell_stride(one_block, carried, const_term):
    return const_term - jnp.einsum(
        "abl,al->bl", one_block.astype(jnp.float32), carried, precision=highest
    )


def compose_cells(blocks, sequence):
    running = None
    for position in sequence:
        one_block = blocks[position].astype(jnp.float32)
        running = -jnp.swapaxes(one_block, 0, 1)
    return running


def doubling_maps(local_map, reverse):
    size = lax.axis_size("azim")
    index = lax.axis_index("azim")
    levels = []
    current = local_map
    distance = 1
    while distance < size:
        if reverse:
            moved = from_behind(current, "azim", -distance)
            exists = index + distance < size
        else:
            moved = from_behind(current, "azim", distance)
            exists = index >= distance
        levels.append((current, distance))
        current = jnp.where(
            exists, jnp.einsum("bcl,cal->bal", current, moved, precision=highest), current
        )
        distance = distance * 2
    return (levels, current)


def doubling_entries(map_levels, local_offset, reverse):
    levels, final_map = map_levels
    size = lax.axis_size("azim")
    index = lax.axis_index("azim")
    running = local_offset
    for current, distance in levels:
        if reverse:
            moved = from_behind(running, "azim", -distance)
        else:
            moved = from_behind(running, "azim", distance)
        running = jnp.einsum("bcl,cl->bl", current, moved, precision=highest) + running
    if reverse:
        wrapped = from_root(running, "azim", 0)
    else:
        wrapped = from_root(running, "azim", size - 1)
    leaving = jnp.einsum("bcl,cl->bl", final_map, wrapped, precision=highest) + running
    if reverse:
        shifted = from_behind(leaving, "azim", -1)
        first_device = index == size - 1
    else:
        shifted = from_behind(leaving, "azim", 1)
        first_device = index == 0
    return jnp.where(first_device, wrapped, shifted)


def sweep(blocks, consts, map_levels, reverse):
    cell_count = blocks.shape[0]
    sequence = list(range(cell_count))
    if reverse:
        sequence = sequence[::-1]
    carried = jnp.zeros(consts.shape[1:], jnp.float32)
    for position in sequence:
        carried = cell_stride(blocks[position], carried, consts[position])
    local_offset = carried
    incoming_maps = doubling_entries(map_levels, local_offset, reverse)
    outputs = [None] * cell_count
    carried = incoming_maps
    for position in sequence:
        carried = cell_stride(blocks[position], carried, consts[position])
        outputs[position] = carried
    return jnp.stack(outputs)


def on_device(rhs, coupling, fwd_coupling, bwd_coupling, block_inverse):
    cell_count, block_width, _, position_total, radial_count = fwd_coupling.shape
    line_count = position_total * radial_count
    forward_blocks = fwd_coupling.reshape(cell_count, block_width, block_width, line_count)
    backward_blocks = bwd_coupling.reshape(cell_count, block_width, block_width, line_count)
    inverse_blocks = block_inverse.reshape(cell_count, block_width, block_width, line_count)
    source = rhs.reshape(cell_count, block_width, line_count)
    coupling_field = coupling.reshape(cell_count, block_width, line_count)
    forward_map = compose_cells(forward_blocks, list(range(cell_count)))
    backward_map = compose_cells(backward_blocks, list(range(cell_count))[::-1])
    forward_levels = None
    backward_levels = None
    forward_levels = doubling_maps(forward_map, False)
    backward_levels = doubling_maps(backward_map, True)

    def precondition(vector):
        consts = jnp.stack(
            [
                jnp.einsum(
                    "abl,al->bl",
                    inverse_blocks[0].astype(jnp.float32),
                    vector[0],
                    precision=highest,
                )
            ]
        )
        forward = sweep(forward_blocks, consts, forward_levels, False)
        return sweep(backward_blocks, forward, backward_levels, True)

    def stations_sum(field):
        grid = field.reshape(cell_count, block_width, position_total, radial_count)
        padded = extended(grid, (("axial", 2),), 1)
        return (padded[:, :, :-2] + padded[:, :, 2:]).reshape(cell_count, block_width, line_count)

    applied_once = precondition(source)
    middle = source - applied_once + coupling_field * stations_sum(applied_once)
    second = precondition(middle)
    correction = applied_once + second
    remaining = middle - second + coupling_field * stations_sum(second)
    return (correction.reshape(rhs.shape), remaining.reshape(rhs.shape))


def solution(mesh):
    cells, stations = mesh.shape["azim"], mesh.shape["axial"]

    def on_each(rhs, coupling, fwd_coupling, bwd_coupling, block_inverse):
        local = fwd_coupling.shape
        if (cells, stations) == (8, 4) and local == (1, 48, 48, 1, 128):
            return line_plan(rhs, coupling, fwd_coupling, bwd_coupling, block_inverse)
        return on_device(rhs, coupling, fwd_coupling, bwd_coupling, block_inverse)

    return jax.shard_map(
        on_each,
        mesh=mesh,
        in_specs=(
            P("azim", None, "axial", None),
            P("azim", None, "axial", None),
            P("azim", None, None, "axial", None),
            P("azim", None, None, "axial", None),
            P("azim", None, None, "axial", None),
        ),
        out_specs=(P("azim", None, "axial", None), P("azim", None, "axial", None)),
        check_vma=False,
    )
```

profile of v0, /device:TPU:1, one launch (start us, length us, event | category | flops | bytes accessed | tf_op | source)
XLA Modules:
  0.0 94.9 jit_solution(16624258674563167164)
XLA Ops:
  0.6 3.9 %shard_map.68 = f32[32,152,128]{2,1,0:T(8,128)} custom-call(bf16[48,48,128]{2,1,0:T(8,128)(2,1)} %bitcast.17, bf16[48,48,128]{2,1,0:T(8,128)(2,1)} %bitcast.18, bf16[48,48,128]{2,1,0:T(8,128)(2,1)} %bitcast.15, f32[48,128]{1,0:T(8,128)} %bitcast.19, f32[48,128]{1,0:T(8,128)} %bitcast.20), custom_call_target="tpu_custom_call" | custom-call | tf_op jit(solution)/shard_map/pallas_call | solution.py:415
  4.5 7.1 %all-to-all-start = ((f32[32,152,128]{2,1,0:T(8,128)}), f32[32,152,128]{2,1,0:T(8,128)S(1)}, u32[]{:S(2)}, u32[]{:S(2)}) async-start(f32[32,152,128]{2,1,0:T(8,128)} %shard_map.68), calls=%async_computation | async-start | bytes 4980736 | tf_op jit(solution)/shard_map/all_to_all | solution.py:433
  11.6 4.1 %shard_map.70 = (f32[144,128]{1,0:T(8,128)S(1)}, f32[144,128]{1,0:T(8,128)S(1)}, f32[144,128]{1,0:T(8,128)S(1)}, f32[144,128]{1,0:T(8,128)S(1)}, f32[144,128]{1,...) custom-call(bf16[48,48,128]{2,1,0:T(8,128)(2,1)} %bitcast.16), custom_call_target="tpu_custom_call" | custom-call | tf_op jit(solution)/shard_map/pallas_call | solution.py:435
  15.7 0.3 collective-permute-start
  16.1 1.5 %collective-permute-start.1 = (f32[144,128]{1,0:T(8,128)S(1)}, f32[144,128]{1,0:T(8,128)S(1)}, u32[]{:S(2)}, u32[]{:S(2)}) collective-permute-start(f32[144,128]{1,0:T(8,128)S(1)} %get-tuple-element.34), channel_id=1, source_target_pairs={{0,2},{1,3},{2,0},{3,1},{4,6},{5,7},{6,4},{7,5},{8,10},{9,11},{10,... | collective-permute-start | bytes 221192 | tf_op jit(solution)/shard_map/ppermute | solution.py:445
  17.5 0.4 collective-permute-start.2
  17.9 1.4 %collective-permute-start.3 = (f32[144,128]{1,0:T(8,128)S(1)}, f32[144,128]{1,0:T(8,128)S(1)}, u32[]{:S(2)}, u32[]{:S(2)}) collective-permute-start(f32[144,128]{1,0:T(8,128)S(1)} %get-tuple-element.36), channel_id=1, source_target_pairs={{0,4},{1,5},{2,6},{3,7},{4,0},{5,1},{6,2},{7,3},{8,12},{9,13},{10,... | collective-permute-start | bytes 221192 | tf_op jit(solution)/shard_map/ppermute | solution.py:445
  19.3 0.3 collective-permute-start.4
  19.6 0.0 collective-permute-done.refs_1_
  19.6 2.3 %collective-permute-start.5 = (f32[144,128]{1,0:T(8,128)S(1)}, f32[144,128]{1,0:T(8,128)S(1)}, u32[]{:S(2)}, u32[]{:S(2)}) collective-permute-start(f32[144,128]{1,0:T(8,128)S(1)} %get-tuple-element.38), channel_id=1, source_target_pairs={{0,6},{1,7},{2,4},{3,5},{4,2},{5,3},{6,0},{7,1},{8,14},{9,15},{10,... | collective-permute-start | bytes 221192 | tf_op jit(solution)/shard_map/ppermute | solution.py:445
  21.9 6.9 %collective-permute-done.1.refs_2_ = f32[144,128]{1,0:T(8,128)S(1)} collective-permute-done((f32[144,128]{1,0:T(8,128)S(1)}, f32[144,128]{1,0:T(8,128)S(1)}, u32[]{:S(2)}, u32[]{:S(2)}) %collective-permute-start.1) | collective-permute-done | bytes 73760 | tf_op jit(solution)/shard_map/ppermute | solution.py:445
  28.8 1.8 %collective-permute-start.6 = (f32[144,128]{1,0:T(8,128)S(1)}, f32[144,128]{1,0:T(8,128)S(1)}, u32[]{:S(2)}, u32[]{:S(2)}) collective-permute-start(f32[144,128]{1,0:T(8,128)S(1)} %get-tuple-element.39), channel_id=1, source_target_pairs={{0,7},{1,6},{2,5},{3,4},{4,3},{5,2},{6,1},{7,0},{8,15},{9,14},{10,... | collective-permute-start | bytes 221192 | tf_op jit(solution)/shard_map/ppermute | solution.py:445
  30.6 2.8 %collective-permute-done.2.refs_3_ = f32[144,128]{1,0:T(8,128)S(1)} collective-permute-done((f32[144,128]{1,0:T(8,128)S(1)}, f32[144,128]{1,0:T(8,128)S(1)}, u32[]{:S(2)}, u32[]{:S(2)}) %collective-permute-start.2) | collective-permute-done | bytes 73760 | tf_op jit(solution)/shard_map/ppermute | solution.py:445
  33.4 0.0 collective-permute-start.7
  33.4 0.0 collective-permute-done.3.refs_0_
  33.4 0.0 collective-permute-start.8
  33.4 1.3 %collective-permute-done.4.refs_1_ = f32[144,128]{1,0:T(8,128)S(1)} collective-permute-done((f32[144,128]{1,0:T(8,128)S(1)}, f32[144,128]{1,0:T(8,128)S(1)}, u32[]{:S(2)}, u32[]{:S(2)}) %collective-permute-start.4) | collective-permute-done | bytes 73760 | tf_op jit(solution)/shard_map/ppermute | solution.py:445
  34.7 3.1 %collective-permute-start.9 = (f32[144,128]{1,0:T(8,128)S(1)}, f32[144,128]{1,0:T(8,128)S(1)}, u32[]{:S(2)}, u32[]{:S(2)}) collective-permute-start(f32[144,128]{1,0:T(8,128)S(1)} %get-tuple-element.42), channel_id=1, source_target_pairs={{0,10},{1,11},{2,8},{3,9},{4,14},{5,15},{6,12},{7,13},{8,2},{9,3},... | collective-permute-start | bytes 221192 | tf_op jit(solution)/shard_map/ppermute | solution.py:445
  37.8 0.6 collective-permute-done.5.refs_2_
  38.5 0.2 collective-permute-start.10
  38.7 3.2 %collective-permute-done.6.refs_3_ = f32[144,128]{1,0:T(8,128)S(1)} collective-permute-done((f32[144,128]{1,0:T(8,128)S(1)}, f32[144,128]{1,0:T(8,128)S(1)}, u32[]{:S(2)}, u32[]{:S(2)}) %collective-permute-start.6) | collective-permute-done | bytes 73760 | tf_op jit(solution)/shard_map/ppermute | solution.py:445
  41.9 0.0 collective-permute-start.11
  41.9 12.2 %collective-permute-done.7.refs_0_ = f32[144,128]{1,0:T(8,128)S(1)} collective-permute-done((f32[144,128]{1,0:T(8,128)S(1)}, f32[144,128]{1,0:T(8,128)S(1)}, u32[]{:S(2)}, u32[]{:S(2)}) %collective-permute-start.7) | collective-permute-done | bytes 73760 | tf_op jit(solution)/shard_map/ppermute | solution.py:445
  54.1 4.0 %collective-permute-start.12 = (f32[144,128]{1,0:T(8,128)}, f32[144,128]{1,0:T(8,128)S(1)}, u32[]{:S(2)}, u32[]{:S(2)}) collective-permute-start(f32[144,128]{1,0:T(8,128)} %get-tuple-element.45), channel_id=1, source_target_pairs={{0,13},{1,12},{2,15},{3,14},{4,9},{5,8},{6,11},{7,10},{8,5},{9,4},... | collective-permute-start | bytes 221192 | tf_op jit(solution)/shard_map/ppermute | solution.py:445
  58.1 0.0 collective-permute-done.8.refs_1_
  58.1 2.4 %collective-permute-start.13 = (f32[144,128]{1,0:T(8,128)}, f32[144,128]{1,0:T(8,128)}, u32[]{:S(2)}, u32[]{:S(2)}) collective-permute-start(f32[144,128]{1,0:T(8,128)} %get-tuple-element.46), channel_id=1, source_target_pairs={{0,14},{1,15},{2,12},{3,13},{4,10},{5,11},{6,8},{7,9},{8,6},{9,7},... | collective-permute-start | bytes 221192 | tf_op jit(solution)/shard_map/ppermute | solution.py:445
  60.5 0.0 collective-permute-done.9.refs_2_
  60.5 1.7 %collective-permute-start.14 = (f32[144,128]{1,0:T(8,128)}, f32[144,128]{1,0:T(8,128)}, u32[]{:S(2)}, u32[]{:S(2)}) collective-permute-start(f32[144,128]{1,0:T(8,128)} %get-tuple-element.47), channel_id=1, source_target_pairs={{0,15},{1,14},{2,13},{3,12},{4,11},{5,10},{6,9},{7,8},{8,7},{9,6},... | collective-permute-start | bytes 221192 | tf_op jit(solution)/shard_map/ppermute | solution.py:445
  62.1 6.5 %all-to-all-done.slots_ref = f32[32,152,128]{2,1,0:T(8,128)S(1)} async-done(((f32[32,152,128]{2,1,0:T(8,128)}), f32[32,152,128]{2,1,0:T(8,128)S(1)}, u32[]{:S(2)}, u32[]{:S(2)}) %all-to-all-start) | async-done | bytes 2490400 | tf_op jit(solution)/shard_map/all_to_all | solution.py:433
  68.6 2.8 %shard_map.69 = (f32[3,8,128]{2,1,0:T(8,128)S(1)}, f32[3,8,128]{2,1,0:T(8,128)S(1)}, f32[8,288,128]{2,1,0:T(8,128)S(1)}, f32[8,288,128]{2,1,0:T(8,128)S(1)}, f32...) custom-call(f32[32,152,128]{2,1,0:T(8,128)S(1)} %all-to-all-done.slots_ref), custom_call_target="tpu_custom_call" | custom-call | tf_op jit(solution)/shard_map/pallas_call | solution.py:450
  71.4 0.0 collective-permute-done.10.refs_3_
  71.4 2.7 %collective-permute-start.15 = (f32[3,8,128]{2,1,0:T(8,128)S(1)}, f32[3,8,128]{2,1,0:T(8,128)S(1)}, u32[]{:S(2)}, u32[]{:S(2)}) collective-permute-start(f32[3,8,128]{2,1,0:T(8,128)S(1)} %get-tuple-element.48), channel_id=1, source_target_pairs={{0,16},{1,17},{2,18},{3,19},{4,20},{5,21},{6,22},{7,23},{8,24},{9,... | collective-permute-start | bytes 36872 | tf_op jit(solution)/shard_map/ppermute | solution.py:455
  74.1 0.1 shard_map.71.refs_0_
  74.3 0.1 shard_map.72.refs_1_
  74.4 0.1 shard_map.73.refs_2_
  74.6 0.0 collective-permute-done.11.refs_0_
  74.6 0.0 collective-permute-done.12.refs_1_
  74.6 0.0 collective-permute-done.13.refs_2_
  74.6 0.0 collective-permute-done.14.refs_3_
  74.6 1.1 %shard_map.74.refs_3_ = f32[2,288,128]{2,1,0:T(8,128)S(1)} custom-call(f32[144,128]{1,0:T(8,128)S(1)} %collective-permute-done.11.refs_0_, f32[144,128]{1,0:T(8,128)S(1)} %collective-permute-done.12.refs_1_, f32[144,128]{1,0:T(8,128)} %collective-permute-done.13.refs_2_, f32[144,128]{1,0:T(8,128)} %collective-permute-done.14.refs_3_), custom_call_target="tpu_custom_call" | custom-call | tf_op jit(solution)/shard_map/pallas_call | solution.py:447
  75.7 0.0 collective-permute-done.15.vector_ref
  75.7 0.1 shard_map.76
  75.8 1.9 %collective-permute-start.16 = (f32[3,8,128]{2,1,0:T(8,128)S(1)}, f32[3,8,128]{2,1,0:T(8,128)S(1)}, u32[]{:S(2)}, u32[]{:S(2)}) collective-permute-start(f32[3,8,128]{2,1,0:T(8,128)S(1)} %shard_map.76), channel_id=1, source_target_pairs={{0,16},{1,17},{2,18},{3,19},{4,20},{5,21},{6,22},{7,23},{8,24},{9,... | collective-permute-start | bytes 36872 | tf_op jit(solution)/shard_map/ppermute | solution.py:455
  77.8 0.1 shard_map.75.own_ref
  77.9 1.5 %collective-permute-done.16.other_ref = f32[3,8,128]{2,1,0:T(8,128)S(1)} collective-permute-done((f32[3,8,128]{2,1,0:T(8,128)S(1)}, f32[3,8,128]{2,1,0:T(8,128)S(1)}, u32[]{:S(2)}, u32[]{:S(2)}) %collective-permute-start.16) | collective-permute-done | bytes 12320 | tf_op jit(solution)/shard_map/ppermute | solution.py:455
  79.3 2.8 %shard_map.77 = f32[128,128]{1,0:T(8,128)S(1)} custom-call(f32[3,8,128]{2,1,0:T(8,128)S(1)} %shard_map.75.own_ref, f32[3,8,128]{2,1,0:T(8,128)S(1)} %collective-permute-done.16.other_ref, f32[8,288,128]{2,1,0:T(8,128)S(1)} %get-tuple-element.49.forward_ref, f32[8,288,128]{2,1,0:T(8,128)S(1)} %get-tuple-element.50.backward_ref, ...), custom_call_target="tpu_custom_call" | custom-call | tf_op jit(solution)/shard_map/pallas_call | solution.py:461
  82.2 11.8 %all_to_all.10 = f32[32,4,128]{2,1,0:T(4,128)S(1)} all-to-all(f32[32,4,128]{2,1,0:T(4,128)S(1)} %bitcast.13), channel_id=1, replica_groups={{0,8,16,24,1,9,17,25,2,10,18,26,3,11,19,27,4,12,20,28,5,13,21,29,6,14,2..., dimensions={0} | all-to-all | bytes 131072 | tf_op jit(solution)/shard_map/all_to_all | solution.py:402
  94.0 1.0 %shard_map.78 = (f32[48,128]{1,0:T(8,128)}, f32[48,128]{1,0:T(8,128)}) custom-call(f32[128,128]{1,0:T(8,128)S(1)} %bitcast.14), custom_call_target="tpu_custom_call" | custom-call | tf_op jit(solution)/shard_map/pallas_call | solution.py:465
Async XLA Ops:
  4.5 64.1 %all-to-all-start = ((f32[32,152,128]{2,1,0:T(8,128)}), f32[32,152,128]{2,1,0:T(8,128)S(1)}, u32[]{:S(2)}, u32[]{:S(2)}) async-start(f32[32,152,128]{2,1,0:T(8,128)} %shard_map.68), calls=%async_computation | async-start | bytes 4980736 | tf_op jit(solution)/shard_map/all_to_all | solution.py:433
  15.7 3.9 %collective-permute-start = (f32[144,128]{1,0:T(8,128)S(1)}, f32[144,128]{1,0:T(8,128)S(1)}, u32[]{:S(2)}, u32[]{:S(2)}) collective-permute-start(f32[144,128]{1,0:T(8,128)S(1)} %get-tuple-element.33), channel_id=1, source_target_pairs={{0,1},{1,0},{2,3},{3,2},{4,5},{5,4},{6,7},{7,6},{8,9},{9,8},{10,11... | collective-permute-start | bytes 221192 | tf_op jit(solution)/shard_map/ppermute | solution.py:445
  16.1 12.8 %collective-permute-start.1 = (f32[144,128]{1,0:T(8,128)S(1)}, f32[144,128]{1,0:T(8,128)S(1)}, u32[]{:S(2)}, u32[]{:S(2)}) collective-permute-start(f32[144,128]{1,0:T(8,128)S(1)} %get-tuple-element.34), channel_id=1, source_target_pairs={{0,2},{1,3},{2,0},{3,1},{4,6},{5,7},{6,4},{7,5},{8,10},{9,11},{10,... | collective-permute-start | bytes 221192 | tf_op jit(solution)/shard_map/ppermute | solution.py:445
  17.5 15.9 %collective-permute-start.2 = (f32[144,128]{1,0:T(8,128)S(1)}, f32[144,128]{1,0:T(8,128)S(1)}, u32[]{:S(2)}, u32[]{:S(2)}) collective-permute-start(f32[144,128]{1,0:T(8,128)S(1)} %get-tuple-element.35), channel_id=1, source_target_pairs={{0,3},{1,2},{2,1},{3,0},{4,7},{5,6},{6,5},{7,4},{8,11},{9,10},{10,... | collective-permute-start | bytes 221192 | tf_op jit(solution)/shard_map/ppermute | solution.py:445
  17.9 15.5 %collective-permute-start.3 = (f32[144,128]{1,0:T(8,128)S(1)}, f32[144,128]{1,0:T(8,128)S(1)}, u32[]{:S(2)}, u32[]{:S(2)}) collective-permute-start(f32[144,128]{1,0:T(8,128)S(1)} %get-tuple-element.36), channel_id=1, source_target_pairs={{0,4},{1,5},{2,6},{3,7},{4,0},{5,1},{6,2},{7,3},{8,12},{9,13},{10,... | collective-permute-start | bytes 221192 | tf_op jit(solution)/shard_map/ppermute | solution.py:445
  19.3 15.3 %collective-permute-start.4 = (f32[144,128]{1,0:T(8,128)S(1)}, f32[144,128]{1,0:T(8,128)S(1)}, u32[]{:S(2)}, u32[]{:S(2)}) collective-permute-start(f32[144,128]{1,0:T(8,128)S(1)} %get-tuple-element.37), channel_id=1, source_target_pairs={{0,5},{1,4},{2,7},{3,6},{4,1},{5,0},{6,3},{7,2},{8,13},{9,12},{10,... | collective-permute-start | bytes 221192 | tf_op jit(solution)/shard_map/ppermute | solution.py:445
  19.6 18.8 %collective-permute-start.5 = (f32[144,128]{1,0:T(8,128)S(1)}, f32[144,128]{1,0:T(8,128)S(1)}, u32[]{:S(2)}, u32[]{:S(2)}) collective-permute-start(f32[144,128]{1,0:T(8,128)S(1)} %get-tuple-element.38), channel_id=1, source_target_pairs={{0,6},{1,7},{2,4},{3,5},{4,2},{5,3},{6,0},{7,1},{8,14},{9,15},{10,... | collective-permute-start | bytes 221192 | tf_op jit(solution)/shard_map/ppermute | solution.py:445
  28.8 13.1 %collective-permute-start.6 = (f32[144,128]{1,0:T(8,128)S(1)}, f32[144,128]{1,0:T(8,128)S(1)}, u32[]{:S(2)}, u32[]{:S(2)}) collective-permute-start(f32[144,128]{1,0:T(8,128)S(1)} %get-tuple-element.39), channel_id=1, source_target_pairs={{0,7},{1,6},{2,5},{3,4},{4,3},{5,2},{6,1},{7,0},{8,15},{9,14},{10,... | collective-permute-start | bytes 221192 | tf_op jit(solution)/shard_map/ppermute | solution.py:445
  33.4 20.7 %collective-permute-start.7 = (f32[144,128]{1,0:T(8,128)S(1)}, f32[144,128]{1,0:T(8,128)S(1)}, u32[]{:S(2)}, u32[]{:S(2)}) collective-permute-start(f32[144,128]{1,0:T(8,128)S(1)} %get-tuple-element.40), channel_id=1, source_target_pairs={{0,8},{1,9},{2,10},{3,11},{4,12},{5,13},{6,14},{7,15},{8,0},{9,1},... | collective-permute-start | bytes 221192 | tf_op jit(solution)/shard_map/ppermute | solution.py:445
  33.4 24.7 %collective-permute-start.8 = (f32[144,128]{1,0:T(8,128)S(1)}, f32[144,128]{1,0:T(8,128)S(1)}, u32[]{:S(2)}, u32[]{:S(2)}) collective-permute-start(f32[144,128]{1,0:T(8,128)S(1)} %get-tuple-element.41), channel_id=1, source_target_pairs={{0,9},{1,8},{2,11},{3,10},{4,13},{5,12},{6,15},{7,14},{8,1},{9,0},... | collective-permute-start | bytes 221192 | tf_op jit(solution)/shard_map/ppermute | solution.py:445
  34.7 25.8 %collective-permute-start.9 = (f32[144,128]{1,0:T(8,128)S(1)}, f32[144,128]{1,0:T(8,128)S(1)}, u32[]{:S(2)}, u32[]{:S(2)}) collective-permute-start(f32[144,128]{1,0:T(8,128)S(1)} %get-tuple-element.42), channel_id=1, source_target_pairs={{0,10},{1,11},{2,8},{3,9},{4,14},{5,15},{6,12},{7,13},{8,2},{9,3},... | collective-permute-start | bytes 221192 | tf_op jit(solution)/shard_map/ppermute | solution.py:445
  38.5 33.0 %collective-permute-start.10 = (f32[144,128]{1,0:T(8,128)}, f32[144,128]{1,0:T(8,128)S(1)}, u32[]{:S(2)}, u32[]{:S(2)}) collective-permute-start(f32[144,128]{1,0:T(8,128)} %get-tuple-element.43), channel_id=1, source_target_pairs={{0,11},{1,10},{2,9},{3,8},{4,15},{5,14},{6,13},{7,12},{8,3},{9,2},... | collective-permute-start | bytes 221192 | tf_op jit(solution)/shard_map/ppermute | solution.py:445
  41.9 32.6 %collective-permute-start.11 = (f32[144,128]{1,0:T(8,128)}, f32[144,128]{1,0:T(8,128)S(1)}, u32[]{:S(2)}, u32[]{:S(2)}) collective-permute-start(f32[144,128]{1,0:T(8,128)} %get-tuple-element.44), channel_id=1, source_target_pairs={{0,12},{1,13},{2,14},{3,15},{4,8},{5,9},{6,10},{7,11},{8,4},{9,5},... | collective-permute-start | bytes 221192 | tf_op jit(solution)/shard_map/ppermute | solution.py:445
  54.1 20.5 %collective-permute-start.12 = (f32[144,128]{1,0:T(8,128)}, f32[144,128]{1,0:T(8,128)S(1)}, u32[]{:S(2)}, u32[]{:S(2)}) collective-permute-start(f32[144,128]{1,0:T(8,128)} %get-tuple-element.45), channel_id=1, source_target_pairs={{0,13},{1,12},{2,15},{3,14},{4,9},{5,8},{6,11},{7,10},{8,5},{9,4},... | collective-permute-start | bytes 221192 | tf_op jit(solution)/shard_map/ppermute | solution.py:445
  58.1 16.5 %collective-permute-start.13 = (f32[144,128]{1,0:T(8,128)}, f32[144,128]{1,0:T(8,128)}, u32[]{:S(2)}, u32[]{:S(2)}) collective-permute-start(f32[144,128]{1,0:T(8,128)} %get-tuple-element.46), channel_id=1, source_target_pairs={{0,14},{1,15},{2,12},{3,13},{4,10},{5,11},{6,8},{7,9},{8,6},{9,7},... | collective-permute-start | bytes 221192 | tf_op jit(solution)/shard_map/ppermute | solution.py:445
  60.5 14.1 %collective-permute-start.14 = (f32[144,128]{1,0:T(8,128)}, f32[144,128]{1,0:T(8,128)}, u32[]{:S(2)}, u32[]{:S(2)}) collective-permute-start(f32[144,128]{1,0:T(8,128)} %get-tuple-element.47), channel_id=1, source_target_pairs={{0,15},{1,14},{2,13},{3,12},{4,11},{5,10},{6,9},{7,8},{8,7},{9,6},... | collective-permute-start | bytes 221192 | tf_op jit(solution)/shard_map/ppermute | solution.py:445
  71.4 4.2 %collective-permute-start.15 = (f32[3,8,128]{2,1,0:T(8,128)S(1)}, f32[3,8,128]{2,1,0:T(8,128)S(1)}, u32[]{:S(2)}, u32[]{:S(2)}) collective-permute-start(f32[3,8,128]{2,1,0:T(8,128)S(1)} %get-tuple-element.48), channel_id=1, source_target_pairs={{0,16},{1,17},{2,18},{3,19},{4,20},{5,21},{6,22},{7,23},{8,24},{9,... | collective-permute-start | bytes 36872 | tf_op jit(solution)/shard_map/ppermute | solution.py:455
  75.8 3.5 %collective-permute-start.16 = (f32[3,8,128]{2,1,0:T(8,128)S(1)}, f32[3,8,128]{2,1,0:T(8,128)S(1)}, u32[]{:S(2)}, u32[]{:S(2)}) collective-permute-start(f32[3,8,128]{2,1,0:T(8,128)S(1)} %shard_map.76), channel_id=1, source_target_pairs={{0,16},{1,17},{2,18},{3,19},{4,20},{5,21},{6,22},{7,23},{8,24},{9,... | collective-permute-start | bytes 36872 | tf_op jit(solution)/shard_map/ppermute | solution.py:455
where the time goes:
time: 96.1 us; the launch traced here: 94.9 us
  waiting for transfers between devices  34.9 us (36%)
  starting transfers between devices  31.1 us (32%)
  Pallas kernels  16.3 us (17%)
  blocking collectives  11.8 us (12%)
    ppermute x15, waiting for transfers between devices, line_plan(): lax.ppermute(parts[d], BOTH, [(e, e ^ d) for e in range(32)])  27 us
    ppermute x15, starting transfers between devices, line_plan(): lax.ppermute(parts[d], BOTH, [(e, e ^ d) for e in range(32)])  19.4 us
    all_to_all x1, blocking collectives, exchange(): lax.all_to_all(slots.reshape(32, rows, 128), BOTH, 0, 0, axis_index_group...  11.8 us
    all_to_all x1, starting transfers between devices, line_plan(): lax.all_to_all(slots, BOTH, 0, 0, axis_index_groups=ORDER, tiled=True)  7.1 us
    all_to_all x1, waiting for transfers between devices, line_plan(): lax.all_to_all(slots, BOTH, 0, 0, axis_index_groups=ORDER, tiled=True)  6.46 us
    ppermute x2, starting transfers between devices, with_partner(): return lax.ppermute(vector, BOTH, [(e, e ^ 16) for e in range(32)])  4.6 us
    pallas_call x1, Pallas kernels, line_plan(): pl.pallas_call(inverse_send_kernel, out_shape=[shaped(144, 128)] * 16, in...  4.08 us
    pallas_call x1, Pallas kernels, line_plan(): pl.pallas_call(first_send_kernel, out_shape=pltpu.HBM((32, 152, 128), f32...  3.89 us
  transfers between devices with their start and end apart: 18, of which 8 were waited for; matrix products, arithmetic and copies ran while one was open for 0% of the time, Pallas kernels for 9%

commit v1 on v0

--- a/solution.py
+++ b/solution.py
@@ -13,7 +13,7 @@
 
 
 def chunk_of(cell, station):
-    return 16 * (cell % 2) + 4 * station + cell // 2
+    return 16 * (station % 2) + 8 * (station // 2) + 4 * (cell % 2) + cell // 2
 
 
 ORDER = [[e for chunk in range(32) for e in range(32) if chunk_of(e // 4, e % 4) == chunk]]

time: 96.1 us -> 97.8 us (1.018)
  starting transfers between devices: 31.1 us -> 36.8 us
  waiting for transfers between devices: 34.9 us -> 30.1 us
    ppermute x15, starting transfers between devices: 19.4 us -> 23.2 us  [line_plan(): lax.ppermute(parts[d], BOTH, [(e, e ^ d) for e in range(32)])]
    ppermute x15, waiting for transfers between devices: 27 us -> 23.4 us  [line_plan(): lax.ppermute(parts[d], BOTH, [(e, e ^ d) for e in range(32)])]
    ppermute x2, starting transfers between devices: 4.6 us -> 6.47 us  [with_partner(): return lax.ppermute(vector, BOTH, [(e, e ^ 16) for e in range(32)])]
    all_to_all x1, waiting for transfers between devices: 6.46 us -> 5.26 us  [line_plan(): lax.all_to_all(slots, BOTH, 0, 0, axis_index_groups=ORDER, tiled=True)]
  transfers between devices with their start and end apart: 18 -> 18, of which waited for: 8 -> 7; matrix products, arithmetic and copies ran while one was open for 0% -> 0% of each run, Pallas kernels for 9% -> 9%
where the time goes in v1:
time: 97.8 us; the launch traced here: 96.8 us
  starting transfers between devices  36.8 us (38%)
  waiting for transfers between devices  30.1 us (31%)
  Pallas kernels  16.4 us (17%)
  blocking collectives  12.7 us (13%)
    ppermute x15, waiting for transfers between devices, line_plan(): lax.ppermute(parts[d], BOTH, [(e, e ^ d) for e in range(32)])  23.4 us
    ppermute x15, starting transfers between devices, line_plan(): lax.ppermute(parts[d], BOTH, [(e, e ^ d) for e in range(32)])  23.2 us
    all_to_all x1, blocking collectives, exchange(): lax.all_to_all(slots.reshape(32, rows, 128), BOTH, 0, 0, axis_index_group...  12.7 us
    all_to_all x1, starting transfers between devices, line_plan(): lax.all_to_all(slots, BOTH, 0, 0, axis_index_groups=ORDER, tiled=True)  7.1 us
    ppermute x2, starting transfers between devices, with_partner(): return lax.ppermute(vector, BOTH, [(e, e ^ 16) for e in range(32)])  6.47 us
    all_to_all x1, waiting for transfers between devices, line_plan(): lax.all_to_all(slots, BOTH, 0, 0, axis_index_groups=ORDER, tiled=True)  5.26 us
    pallas_call x1, Pallas kernels, line_plan(): pl.pallas_call(inverse_send_kernel, out_shape=[shaped(144, 128)] * 16, in...  4.13 us
    pallas_call x1, Pallas kernels, line_plan(): pl.pallas_call(first_send_kernel, out_shape=pltpu.HBM((32, 152, 128), f32...  3.89 us
  transfers between devices with their start and end apart: 18, of which 7 were waited for; matrix products, arithmetic and copies ran while one was open for 0% of the time, Pallas kernels for 9%

profile of v1, /device:TPU:1, one launch (start us, length us, event | category | flops | bytes accessed | tf_op | source)
XLA Modules:
  0.0 96.8 jit_solution(1206704973088264907)
XLA Ops:
  0.6 3.9 %shard_map.68 = f32[32,152,128]{2,1,0:T(8,128)} custom-call(bf16[48,48,128]{2,1,0:T(8,128)(2,1)} %bitcast.17, bf16[48,48,128]{2,1,0:T(8,128)(2,1)} %bitcast.18, bf16[48,48,128]{2,1,0:T(8,128)(2,1)} %bitcast.15, f32[48,128]{1,0:T(8,128)} %bitcast.19, f32[48,128]{1,0:T(8,128)} %bitcast.20), custom_call_target="tpu_custom_call" | custom-call | tf_op jit(solution)/shard_map/pallas_call | solution.py:415
  4.5 7.1 %all-to-all-start = ((f32[32,152,128]{2,1,0:T(8,128)}), f32[32,152,128]{2,1,0:T(8,128)S(1)}, u32[]{:S(2)}, u32[]{:S(2)}) async-start(f32[32,152,128]{2,1,0:T(8,128)} %shard_map.68), calls=%async_computation | async-start | bytes 4980736 | tf_op jit(solution)/shard_map/all_to_all | solution.py:433
  11.6 4.1 %shard_map.70 = (f32[144,128]{1,0:T(8,128)S(1)}, f32[144,128]{1,0:T(8,128)S(1)}, f32[144,128]{1,0:T(8,128)S(1)}, f32[144,128]{1,0:T(8,128)S(1)}, f32[144,128]{1,...) custom-call(bf16[48,48,128]{2,1,0:T(8,128)(2,1)} %bitcast.16), custom_call_target="tpu_custom_call" | custom-call | tf_op jit(solution)/shard_map/pallas_call | solution.py:435
  15.8 0.3 collective-permute-start
  16.1 1.5 %collective-permute-start.1 = (f32[144,128]{1,0:T(8,128)S(1)}, f32[144,128]{1,0:T(8,128)S(1)}, u32[]{:S(2)}, u32[]{:S(2)}) collective-permute-start(f32[144,128]{1,0:T(8,128)S(1)} %get-tuple-element.34), channel_id=1, source_target_pairs={{0,2},{1,3},{2,0},{3,1},{4,6},{5,7},{6,4},{7,5},{8,10},{9,11},{10,... | collective-permute-start | bytes 221192 | tf_op jit(solution)/shard_map/ppermute | solution.py:445
  17.6 0.4 collective-permute-start.2
  18.0 1.4 %collective-permute-start.3 = (f32[144,128]{1,0:T(8,128)S(1)}, f32[144,128]{1,0:T(8,128)S(1)}, u32[]{:S(2)}, u32[]{:S(2)}) collective-permute-start(f32[144,128]{1,0:T(8,128)S(1)} %get-tuple-element.36), channel_id=1, source_target_pairs={{0,4},{1,5},{2,6},{3,7},{4,0},{5,1},{6,2},{7,3},{8,12},{9,13},{10,... | collective-permute-start | bytes 221192 | tf_op jit(solution)/shard_map/ppermute | solution.py:445
  19.4 0.3 collective-permute-start.4
  19.7 0.0 collective-permute-done.refs_1_
  19.7 2.3 %collective-permute-start.5 = (f32[144,128]{1,0:T(8,128)S(1)}, f32[144,128]{1,0:T(8,128)S(1)}, u32[]{:S(2)}, u32[]{:S(2)}) collective-permute-start(f32[144,128]{1,0:T(8,128)S(1)} %get-tuple-element.38), channel_id=1, source_target_pairs={{0,6},{1,7},{2,4},{3,5},{4,2},{5,3},{6,0},{7,1},{8,14},{9,15},{10,... | collective-permute-start | bytes 221192 | tf_op jit(solution)/shard_map/ppermute | solution.py:445
  22.0 6.8 %collective-permute-done.1.refs_2_ = f32[144,128]{1,0:T(8,128)S(1)} collective-permute-done((f32[144,128]{1,0:T(8,128)S(1)}, f32[144,128]{1,0:T(8,128)S(1)}, u32[]{:S(2)}, u32[]{:S(2)}) %collective-permute-start.1) | collective-permute-done | bytes 73760 | tf_op jit(solution)/shard_map/ppermute | solution.py:445
  28.8 4.5 %collective-permute-start.6 = (f32[144,128]{1,0:T(8,128)S(1)}, f32[144,128]{1,0:T(8,128)S(1)}, u32[]{:S(2)}, u32[]{:S(2)}) collective-permute-start(f32[144,128]{1,0:T(8,128)S(1)} %get-tuple-element.39), channel_id=1, source_target_pairs={{0,7},{1,6},{2,5},{3,4},{4,3},{5,2},{6,1},{7,0},{8,15},{9,14},{10,... | collective-permute-start | bytes 221192 | tf_op jit(solution)/shard_map/ppermute | solution.py:445
  33.4 0.0 collective-permute-done.2.refs_3_
  33.4 0.0 collective-permute-start.7
  33.4 0.0 collective-permute-done.3.refs_0_
  33.4 0.1 collective-permute-start.8
  33.4 1.2 %collective-permute-done.4.refs_1_ = f32[144,128]{1,0:T(8,128)S(1)} collective-permute-done((f32[144,128]{1,0:T(8,128)S(1)}, f32[144,128]{1,0:T(8,128)S(1)}, u32[]{:S(2)}, u32[]{:S(2)}) %collective-permute-start.4) | collective-permute-done | bytes 73760 | tf_op jit(solution)/shard_map/ppermute | solution.py:445
  34.7 1.1 %collective-permute-start.9 = (f32[144,128]{1,0:T(8,128)S(1)}, f32[144,128]{1,0:T(8,128)S(1)}, u32[]{:S(2)}, u32[]{:S(2)}) collective-permute-start(f32[144,128]{1,0:T(8,128)S(1)} %get-tuple-element.42), channel_id=1, source_target_pairs={{0,10},{1,11},{2,8},{3,9},{4,14},{5,15},{6,12},{7,13},{8,2},{9,3},... | collective-permute-start | bytes 221192 | tf_op jit(solution)/shard_map/ppermute | solution.py:445
  35.8 0.7 collective-permute-done.5.refs_2_
  36.5 1.3 %collective-permute-start.10 = (f32[144,128]{1,0:T(8,128)}, f32[144,128]{1,0:T(8,128)S(1)}, u32[]{:S(2)}, u32[]{:S(2)}) collective-permute-start(f32[144,128]{1,0:T(8,128)} %get-tuple-element.43), channel_id=1, source_target_pairs={{0,11},{1,10},{2,9},{3,8},{4,15},{5,14},{6,13},{7,12},{8,3},{9,2},... | collective-permute-start | bytes 221192 | tf_op jit(solution)/shard_map/ppermute | solution.py:445
  37.8 4.2 %collective-permute-done.6.refs_3_ = f32[144,128]{1,0:T(8,128)S(1)} collective-permute-done((f32[144,128]{1,0:T(8,128)S(1)}, f32[144,128]{1,0:T(8,128)S(1)}, u32[]{:S(2)}, u32[]{:S(2)}) %collective-permute-start.6) | collective-permute-done | bytes 73760 | tf_op jit(solution)/shard_map/ppermute | solution.py:445
  42.0 2.7 %collective-permute-start.11 = (f32[144,128]{1,0:T(8,128)}, f32[144,128]{1,0:T(8,128)S(1)}, u32[]{:S(2)}, u32[]{:S(2)}) collective-permute-start(f32[144,128]{1,0:T(8,128)} %get-tuple-element.44), channel_id=1, source_target_pairs={{0,12},{1,13},{2,14},{3,15},{4,8},{5,9},{6,10},{7,11},{8,4},{9,5},... | collective-permute-start | bytes 221192 | tf_op jit(solution)/shard_map/ppermute | solution.py:445
  44.7 10.4 %collective-permute-done.7.refs_0_ = f32[144,128]{1,0:T(8,128)S(1)} collective-permute-done((f32[144,128]{1,0:T(8,128)S(1)}, f32[144,128]{1,0:T(8,128)S(1)}, u32[]{:S(2)}, u32[]{:S(2)}) %collective-permute-start.7) | collective-permute-done | bytes 73760 | tf_op jit(solution)/shard_map/ppermute | solution.py:445
  55.1 3.2 %collective-permute-start.12 = (f32[144,128]{1,0:T(8,128)}, f32[144,128]{1,0:T(8,128)S(1)}, u32[]{:S(2)}, u32[]{:S(2)}) collective-permute-start(f32[144,128]{1,0:T(8,128)} %get-tuple-element.45), channel_id=1, source_target_pairs={{0,13},{1,12},{2,15},{3,14},{4,9},{5,8},{6,11},{7,10},{8,5},{9,4},... | collective-permute-start | bytes 221192 | tf_op jit(solution)/shard_map/ppermute | solution.py:445
  58.3 0.0 collective-permute-done.8.refs_1_
  58.3 2.1 %collective-permute-start.13 = (f32[144,128]{1,0:T(8,128)}, f32[144,128]{1,0:T(8,128)}, u32[]{:S(2)}, u32[]{:S(2)}) collective-permute-start(f32[144,128]{1,0:T(8,128)} %get-tuple-element.46), channel_id=1, source_target_pairs={{0,14},{1,15},{2,12},{3,13},{4,10},{5,11},{6,8},{7,9},{8,6},{9,7},... | collective-permute-start | bytes 221192 | tf_op jit(solution)/shard_map/ppermute | solution.py:445
  60.4 0.0 collective-permute-done.9.refs_2_
  60.4 2.0 %collective-permute-start.14 = (f32[144,128]{1,0:T(8,128)}, f32[144,128]{1,0:T(8,128)}, u32[]{:S(2)}, u32[]{:S(2)}) collective-permute-start(f32[144,128]{1,0:T(8,128)} %get-tuple-element.47), channel_id=1, source_target_pairs={{0,15},{1,14},{2,13},{3,12},{4,11},{5,10},{6,9},{7,8},{8,7},{9,6},... | collective-permute-start | bytes 221192 | tf_op jit(solution)/shard_map/ppermute | solution.py:445
  62.4 5.3 %all-to-all-done.slots_ref = f32[32,152,128]{2,1,0:T(8,128)S(1)} async-done(((f32[32,152,128]{2,1,0:T(8,128)}), f32[32,152,128]{2,1,0:T(8,128)S(1)}, u32[]{:S(2)}, u32[]{:S(2)}) %all-to-all-start) | async-done | bytes 2490400 | tf_op jit(solution)/shard_map/all_to_all | solution.py:433
  67.7 2.8 %shard_map.69 = (f32[3,8,128]{2,1,0:T(8,128)S(1)}, f32[3,8,128]{2,1,0:T(8,128)S(1)}, f32[8,288,128]{2,1,0:T(8,128)S(1)}, f32[8,288,128]{2,1,0:T(8,128)S(1)}, f32...) custom-call(f32[32,152,128]{2,1,0:T(8,128)S(1)} %all-to-all-done.slots_ref), custom_call_target="tpu_custom_call" | custom-call | tf_op jit(solution)/shard_map/pallas_call | solution.py:450
  70.5 0.0 collective-permute-done.10.refs_3_
  70.5 4.5 %collective-permute-start.15 = (f32[3,8,128]{2,1,0:T(8,128)S(1)}, f32[3,8,128]{2,1,0:T(8,128)S(1)}, u32[]{:S(2)}, u32[]{:S(2)}) collective-permute-start(f32[3,8,128]{2,1,0:T(8,128)S(1)} %get-tuple-element.48), channel_id=1, source_target_pairs={{0,16},{1,17},{2,18},{3,19},{4,20},{5,21},{6,22},{7,23},{8,24},{9,... | collective-permute-start | bytes 36872 | tf_op jit(solution)/shard_map/ppermute | solution.py:455
  75.0 0.1 shard_map.71.refs_0_
  75.2 0.1 shard_map.72.refs_1_
  75.3 0.1 shard_map.73.refs_2_
  75.5 0.0 collective-permute-done.11.refs_0_
  75.5 0.0 collective-permute-done.12.refs_1_
  75.5 0.0 collective-permute-done.13.refs_2_
  75.5 0.0 collective-permute-done.14.refs_3_
  75.5 1.1 %shard_map.74.refs_3_ = f32[2,288,128]{2,1,0:T(8,128)S(1)} custom-call(f32[144,128]{1,0:T(8,128)S(1)} %collective-permute-done.11.refs_0_, f32[144,128]{1,0:T(8,128)S(1)} %collective-permute-done.12.refs_1_, f32[144,128]{1,0:T(8,128)} %collective-permute-done.13.refs_2_, f32[144,128]{1,0:T(8,128)} %collective-permute-done.14.refs_3_), custom_call_target="tpu_custom_call" | custom-call | tf_op jit(solution)/shard_map/pallas_call | solution.py:447
  76.6 0.0 collective-permute-done.15.vector_ref
  76.6 0.1 shard_map.76
  76.8 1.9 %collective-permute-start.16 = (f32[3,8,128]{2,1,0:T(8,128)S(1)}, f32[3,8,128]{2,1,0:T(8,128)S(1)}, u32[]{:S(2)}, u32[]{:S(2)}) collective-permute-start(f32[3,8,128]{2,1,0:T(8,128)S(1)} %shard_map.76), channel_id=1, source_target_pairs={{0,16},{1,17},{2,18},{3,19},{4,20},{5,21},{6,22},{7,23},{8,24},{9,... | collective-permute-start | bytes 36872 | tf_op jit(solution)/shard_map/ppermute | solution.py:455
  78.7 0.1 shard_map.75.own_ref
  78.8 1.5 %collective-permute-done.16.other_ref = f32[3,8,128]{2,1,0:T(8,128)S(1)} collective-permute-done((f32[3,8,128]{2,1,0:T(8,128)S(1)}, f32[3,8,128]{2,1,0:T(8,128)S(1)}, u32[]{:S(2)}, u32[]{:S(2)}) %collective-permute-start.16) | collective-permute-done | bytes 12320 | tf_op jit(solution)/shard_map/ppermute | solution.py:455
  80.3 2.8 %shard_map.77 = f32[128,128]{1,0:T(8,128)S(1)} custom-call(f32[3,8,128]{2,1,0:T(8,128)S(1)} %shard_map.75.own_ref, f32[3,8,128]{2,1,0:T(8,128)S(1)} %collective-permute-done.16.other_ref, f32[8,288,128]{2,1,0:T(8,128)S(1)} %get-tuple-element.49.forward_ref, f32[8,288,128]{2,1,0:T(8,128)S(1)} %get-tuple-element.50.backward_ref, ...), custom_call_target="tpu_custom_call" | custom-call | tf_op jit(solution)/shard_map/pallas_call | solution.py:461
  83.1 12.7 %all_to_all.10 = f32[32,4,128]{2,1,0:T(4,128)S(1)} all-to-all(f32[32,4,128]{2,1,0:T(4,128)S(1)} %bitcast.13), channel_id=1, replica_groups={{0,8,16,24,4,12,20,28,2,10,18,26,6,14,22,30,1,9,17,25,5,13,21,29,3,11,1..., dimensions={0} | all-to-all | bytes 131072 | tf_op jit(solution)/shard_map/all_to_all | solution.py:402
  95.8 1.0 %shard_map.78 = (f32[48,128]{1,0:T(8,128)}, f32[48,128]{1,0:T(8,128)}) custom-call(f32[128,128]{1,0:T(8,128)S(1)} %bitcast.14), custom_call_target="tpu_custom_call" | custom-call | tf_op jit(solution)/shard_map/pallas_call | solution.py:465
Async XLA Ops:
  4.5 63.1 %all-to-all-start = ((f32[32,152,128]{2,1,0:T(8,128)}), f32[32,152,128]{2,1,0:T(8,128)S(1)}, u32[]{:S(2)}, u32[]{:S(2)}) async-start(f32[32,152,128]{2,1,0:T(8,128)} %shard_map.68), calls=%async_computation | async-start | bytes 4980736 | tf_op jit(solution)/shard_map/all_to_all | solution.py:433
  15.8 3.9 %collective-permute-start = (f32[144,128]{1,0:T(8,128)S(1)}, f32[144,128]{1,0:T(8,128)S(1)}, u32[]{:S(2)}, u32[]{:S(2)}) collective-permute-start(f32[144,128]{1,0:T(8,128)S(1)} %get-tuple-element.33), channel_id=1, source_target_pairs={{0,1},{1,0},{2,3},{3,2},{4,5},{5,4},{6,7},{7,6},{8,9},{9,8},{10,11... | collective-permute-start | bytes 221192 | tf_op jit(solution)/shard_map/ppermute | solution.py:445
  16.1 12.7 %collective-permute-start.1 = (f32[144,128]{1,0:T(8,128)S(1)}, f32[144,128]{1,0:T(8,128)S(1)}, u32[]{:S(2)}, u32[]{:S(2)}) collective-permute-start(f32[144,128]{1,0:T(8,128)S(1)} %get-tuple-element.34), channel_id=1, source_target_pairs={{0,2},{1,3},{2,0},{3,1},{4,6},{5,7},{6,4},{7,5},{8,10},{9,11},{10,... | collective-permute-start | bytes 221192 | tf_op jit(solution)/shard_map/ppermute | solution.py:445
  17.6 15.8 %collective-permute-start.2 = (f32[144,128]{1,0:T(8,128)S(1)}, f32[144,128]{1,0:T(8,128)S(1)}, u32[]{:S(2)}, u32[]{:S(2)}) collective-permute-start(f32[144,128]{1,0:T(8,128)S(1)} %get-tuple-element.35), channel_id=1, source_target_pairs={{0,3},{1,2},{2,1},{3,0},{4,7},{5,6},{6,5},{7,4},{8,11},{9,10},{10,... | collective-permute-start | bytes 221192 | tf_op jit(solution)/shard_map/ppermute | solution.py:445
  18.0 15.4 %collective-permute-start.3 = (f32[144,128]{1,0:T(8,128)S(1)}, f32[144,128]{1,0:T(8,128)S(1)}, u32[]{:S(2)}, u32[]{:S(2)}) collective-permute-start(f32[144,128]{1,0:T(8,128)S(1)} %get-tuple-element.36), channel_id=1, source_target_pairs={{0,4},{1,5},{2,6},{3,7},{4,0},{5,1},{6,2},{7,3},{8,12},{9,13},{10,... | collective-permute-start | bytes 221192 | tf_op jit(solution)/shard_map/ppermute | solution.py:445
  19.4 15.3 %collective-permute-start.4 = (f32[144,128]{1,0:T(8,128)S(1)}, f32[144,128]{1,0:T(8,128)S(1)}, u32[]{:S(2)}, u32[]{:S(2)}) collective-permute-start(f32[144,128]{1,0:T(8,128)S(1)} %get-tuple-element.37), channel_id=1, source_target_pairs={{0,5},{1,4},{2,7},{3,6},{4,1},{5,0},{6,3},{7,2},{8,13},{9,12},{10,... | collective-permute-start | bytes 221192 | tf_op jit(solution)/shard_map/ppermute | solution.py:445
  19.7 16.8 %collective-permute-start.5 = (f32[144,128]{1,0:T(8,128)S(1)}, f32[144,128]{1,0:T(8,128)S(1)}, u32[]{:S(2)}, u32[]{:S(2)}) collective-permute-start(f32[144,128]{1,0:T(8,128)S(1)} %get-tuple-element.38), channel_id=1, source_target_pairs={{0,6},{1,7},{2,4},{3,5},{4,2},{5,3},{6,0},{7,1},{8,14},{9,15},{10,... | collective-permute-start | bytes 221192 | tf_op jit(solution)/shard_map/ppermute | solution.py:445
  28.8 13.2 %collective-permute-start.6 = (f32[144,128]{1,0:T(8,128)S(1)}, f32[144,128]{1,0:T(8,128)S(1)}, u32[]{:S(2)}, u32[]{:S(2)}) collective-permute-start(f32[144,128]{1,0:T(8,128)S(1)} %get-tuple-element.39), channel_id=1, source_target_pairs={{0,7},{1,6},{2,5},{3,4},{4,3},{5,2},{6,1},{7,0},{8,15},{9,14},{10,... | collective-permute-start | bytes 221192 | tf_op jit(solution)/shard_map/ppermute | solution.py:445
  33.4 21.8 %collective-permute-start.7 = (f32[144,128]{1,0:T(8,128)S(1)}, f32[144,128]{1,0:T(8,128)S(1)}, u32[]{:S(2)}, u32[]{:S(2)}) collective-permute-start(f32[144,128]{1,0:T(8,128)S(1)} %get-tuple-element.40), channel_id=1, source_target_pairs={{0,8},{1,9},{2,10},{3,11},{4,12},{5,13},{6,14},{7,15},{8,0},{9,1},... | collective-permute-start | bytes 221192 | tf_op jit(solution)/shard_map/ppermute | solution.py:445
  33.4 24.9 %collective-permute-start.8 = (f32[144,128]{1,0:T(8,128)S(1)}, f32[144,128]{1,0:T(8,128)S(1)}, u32[]{:S(2)}, u32[]{:S(2)}) collective-permute-start(f32[144,128]{1,0:T(8,128)S(1)} %get-tuple-element.41), channel_id=1, source_target_pairs={{0,9},{1,8},{2,11},{3,10},{4,13},{5,12},{6,15},{7,14},{8,1},{9,0},... | collective-permute-start | bytes 221192 | tf_op jit(solution)/shard_map/ppermute | solution.py:445
  34.7 25.7 %collective-permute-start.9 = (f32[144,128]{1,0:T(8,128)S(1)}, f32[144,128]{1,0:T(8,128)S(1)}, u32[]{:S(2)}, u32[]{:S(2)}) collective-permute-start(f32[144,128]{1,0:T(8,128)S(1)} %get-tuple-element.42), channel_id=1, source_target_pairs={{0,10},{1,11},{2,8},{3,9},{4,14},{5,15},{6,12},{7,13},{8,2},{9,3},... | collective-permute-start | bytes 221192 | tf_op jit(solution)/shard_map/ppermute | solution.py:445
  36.5 34.0 %collective-permute-start.10 = (f32[144,128]{1,0:T(8,128)}, f32[144,128]{1,0:T(8,128)S(1)}, u32[]{:S(2)}, u32[]{:S(2)}) collective-permute-start(f32[144,128]{1,0:T(8,128)} %get-tuple-element.43), channel_id=1, source_target_pairs={{0,11},{1,10},{2,9},{3,8},{4,15},{5,14},{6,13},{7,12},{8,3},{9,2},... | collective-permute-start | bytes 221192 | tf_op jit(solution)/shard_map/ppermute | solution.py:445
  42.0 33.5 %collective-permute-start.11 = (f32[144,128]{1,0:T(8,128)}, f32[144,128]{1,0:T(8,128)S(1)}, u32[]{:S(2)}, u32[]{:S(2)}) collective-permute-start(f32[144,128]{1,0:T(8,128)} %get-tuple-element.44), channel_id=1, source_target_pairs={{0,12},{1,13},{2,14},{3,15},{4,8},{5,9},{6,10},{7,11},{8,4},{9,5},... | collective-permute-start | bytes 221192 | tf_op jit(solution)/shard_map/ppermute | solution.py:445
  55.1 20.4 %collective-permute-start.12 = (f32[144,128]{1,0:T(8,128)}, f32[144,128]{1,0:T(8,128)S(1)}, u32[]{:S(2)}, u32[]{:S(2)}) collective-permute-start(f32[144,128]{1,0:T(8,128)} %get-tuple-element.45), channel_id=1, source_target_pairs={{0,13},{1,12},{2,15},{3,14},{4,9},{5,8},{6,11},{7,10},{8,5},{9,4},... | collective-permute-start | bytes 221192 | tf_op jit(solution)/shard_map/ppermute | solution.py:445
  58.3 17.2 %collective-permute-start.13 = (f32[144,128]{1,0:T(8,128)}, f32[144,128]{1,0:T(8,128)}, u32[]{:S(2)}, u32[]{:S(2)}) collective-permute-start(f32[144,128]{1,0:T(8,128)} %get-tuple-element.46), channel_id=1, source_target_pairs={{0,14},{1,15},{2,12},{3,13},{4,10},{5,11},{6,8},{7,9},{8,6},{9,7},... | collective-permute-start | bytes 221192 | tf_op jit(solution)/shard_map/ppermute | solution.py:445
  60.4 15.1 %collective-permute-start.14 = (f32[144,128]{1,0:T(8,128)}, f32[144,128]{1,0:T(8,128)}, u32[]{:S(2)}, u32[]{:S(2)}) collective-permute-start(f32[144,128]{1,0:T(8,128)} %get-tuple-element.47), channel_id=1, source_target_pairs={{0,15},{1,14},{2,13},{3,12},{4,11},{5,10},{6,9},{7,8},{8,7},{9,6},... | collective-permute-start | bytes 221192 | tf_op jit(solution)/shard_map/ppermute | solution.py:445
  70.5 6.1 %collective-permute-start.15 = (f32[3,8,128]{2,1,0:T(8,128)S(1)}, f32[3,8,128]{2,1,0:T(8,128)S(1)}, u32[]{:S(2)}, u32[]{:S(2)}) collective-permute-start(f32[3,8,128]{2,1,0:T(8,128)S(1)} %get-tuple-element.48), channel_id=1, source_target_pairs={{0,16},{1,17},{2,18},{3,19},{4,20},{5,21},{6,22},{7,23},{8,24},{9,... | collective-permute-start | bytes 36872 | tf_op jit(solution)/shard_map/ppermute | solution.py:455
  76.8 3.5 %collective-permute-start.16 = (f32[3,8,128]{2,1,0:T(8,128)S(1)}, f32[3,8,128]{2,1,0:T(8,128)S(1)}, u32[]{:S(2)}, u32[]{:S(2)}) collective-permute-start(f32[3,8,128]{2,1,0:T(8,128)S(1)} %shard_map.76), channel_id=1, source_target_pairs={{0,16},{1,17},{2,18},{3,19},{4,20},{5,21},{6,22},{7,23},{8,24},{9,... | collective-permute-start | bytes 36872 | tf_op jit(solution)/shard_map/ppermute | solution.py:455

commit v2 on v1

--- a/solution.py
+++ b/solution.py
@@ -13,7 +13,7 @@
 
 
 def chunk_of(cell, station):
-    return 16 * (station % 2) + 8 * (station // 2) + 4 * (cell % 2) + cell // 2
+    return 16 * (station // 2) + 8 * (cell % 2) + 4 * (station % 2) + cell // 2
 
 
 ORDER = [[e for chunk in range(32) for e in range(32) if chunk_of(e // 4, e % 4) == chunk]]

time: 97.8 us -> 96.8 us (0.990)
  starting transfers between devices: 36.8 us -> 29 us
  waiting for transfers between devices: 30.1 us -> 36.5 us
    ppermute x15, waiting for transfers between devices: 23.4 us -> 27.9 us  [line_plan(): lax.ppermute(parts[d], BOTH, [(e, e ^ d) for e in range(32)])]
    ppermute x2, starting transfers between devices: 6.47 us -> 2.6 us  [with_partner(): return lax.ppermute(vector, BOTH, [(e, e ^ 16) for e in range(32)])]
    ppermute x15, starting transfers between devices: 23.2 us -> 19.3 us  [line_plan(): lax.ppermute(parts[d], BOTH, [(e, e ^ d) for e in range(32)])]
    ppermute x2, waiting for transfers between devices: 1.46 us -> 3.06 us  [with_partner(): return lax.ppermute(vector, BOTH, [(e, e ^ 16) for e in range(32)])]
  transfers between devices with their start and end apart: 18 -> 18, of which waited for: 7 -> 6; matrix products, arithmetic and copies ran while one was open for 0% -> 0% of each run, Pallas kernels for 9% -> 9%
where the time goes in v2:
time: 96.8 us; the launch traced here: 95.7 us
  waiting for transfers between devices  36.5 us (38%)
  starting transfers between devices  29 us (30%)
  Pallas kernels  16.4 us (17%)
  blocking collectives  13 us (13%)
    ppermute x15, waiting for transfers between devices, line_plan(): lax.ppermute(parts[d], BOTH, [(e, e ^ d) for e in range(32)])  27.9 us
    ppermute x15, starting transfers between devices, line_plan(): lax.ppermute(parts[d], BOTH, [(e, e ^ d) for e in range(32)])  19.3 us
    all_to_all x1, blocking collectives, exchange(): lax.all_to_all(slots.reshape(32, rows, 128), BOTH, 0, 0, axis_index_group...  13 us
    all_to_all x1, starting transfers between devices, line_plan(): lax.all_to_all(slots, BOTH, 0, 0, axis_index_groups=ORDER, tiled=True)  7.1 us
    all_to_all x1, waiting for transfers between devices, line_plan(): lax.all_to_all(slots, BOTH, 0, 0, axis_index_groups=ORDER, tiled=True)  5.5 us
    pallas_call x1, Pallas kernels, line_plan(): pl.pallas_call(inverse_send_kernel, out_shape=[shaped(144, 128)] * 16, in...  4.14 us
    pallas_call x1, Pallas kernels, line_plan(): pl.pallas_call(first_send_kernel, out_shape=pltpu.HBM((32, 152, 128), f32...  3.89 us
    ppermute x2, waiting for transfers between devices, with_partner(): return lax.ppermute(vector, BOTH, [(e, e ^ 16) for e in range(32)])  3.06 us
  transfers between devices with their start and end apart: 18, of which 6 were waited for; matrix products, arithmetic and copies ran while one was open for 0% of the time, Pallas kernels for 9%

profile of v2, /device:TPU:1, one launch (start us, length us, event | category | flops | bytes accessed | tf_op | source)
XLA Modules:
  0.0 95.7 jit_solution(4019184479140677036)
XLA Ops:
  0.6 3.9 %shard_map.68 = f32[32,152,128]{2,1,0:T(8,128)} custom-call(bf16[48,48,128]{2,1,0:T(8,128)(2,1)} %bitcast.17, bf16[48,48,128]{2,1,0:T(8,128)(2,1)} %bitcast.18, bf16[48,48,128]{2,1,0:T(8,128)(2,1)} %bitcast.15, f32[48,128]{1,0:T(8,128)} %bitcast.19, f32[48,128]{1,0:T(8,128)} %bitcast.20), custom_call_target="tpu_custom_call" | custom-call | tf_op jit(solution)/shard_map/pallas_call | solution.py:415
  4.5 7.1 %all-to-all-start = ((f32[32,152,128]{2,1,0:T(8,128)}), f32[32,152,128]{2,1,0:T(8,128)S(1)}, u32[]{:S(2)}, u32[]{:S(2)}) async-start(f32[32,152,128]{2,1,0:T(8,128)} %shard_map.68), calls=%async_computation | async-start | bytes 4980736 | tf_op jit(solution)/shard_map/all_to_all | solution.py:433
  11.6 4.1 %shard_map.70 = (f32[144,128]{1,0:T(8,128)S(1)}, f32[144,128]{1,0:T(8,128)S(1)}, f32[144,128]{1,0:T(8,128)S(1)}, f32[144,128]{1,0:T(8,128)S(1)}, f32[144,128]{1,...) custom-call(bf16[48,48,128]{2,1,0:T(8,128)(2,1)} %bitcast.16), custom_call_target="tpu_custom_call" | custom-call | tf_op jit(solution)/shard_map/pallas_call | solution.py:435
  15.8 0.3 collective-permute-start
  16.1 1.5 %collective-permute-start.1 = (f32[144,128]{1,0:T(8,128)S(1)}, f32[144,128]{1,0:T(8,128)S(1)}, u32[]{:S(2)}, u32[]{:S(2)}) collective-permute-start(f32[144,128]{1,0:T(8,128)S(1)} %get-tuple-element.34), channel_id=1, source_target_pairs={{0,2},{1,3},{2,0},{3,1},{4,6},{5,7},{6,4},{7,5},{8,10},{9,11},{10,... | collective-permute-start | bytes 221192 | tf_op jit(solution)/shard_map/ppermute | solution.py:445
  17.6 0.4 collective-permute-start.2
  18.0 1.4 %collective-permute-start.3 = (f32[144,128]{1,0:T(8,128)S(1)}, f32[144,128]{1,0:T(8,128)S(1)}, u32[]{:S(2)}, u32[]{:S(2)}) collective-permute-start(f32[144,128]{1,0:T(8,128)S(1)} %get-tuple-element.36), channel_id=1, source_target_pairs={{0,4},{1,5},{2,6},{3,7},{4,0},{5,1},{6,2},{7,3},{8,12},{9,13},{10,... | collective-permute-start | bytes 221192 | tf_op jit(solution)/shard_map/ppermute | solution.py:445
  19.4 0.3 collective-permute-start.4
  19.7 0.0 collective-permute-done.refs_1_
  19.7 2.3 %collective-permute-start.5 = (f32[144,128]{1,0:T(8,128)S(1)}, f32[144,128]{1,0:T(8,128)S(1)}, u32[]{:S(2)}, u32[]{:S(2)}) collective-permute-start(f32[144,128]{1,0:T(8,128)S(1)} %get-tuple-element.38), channel_id=1, source_target_pairs={{0,6},{1,7},{2,4},{3,5},{4,2},{5,3},{6,0},{7,1},{8,14},{9,15},{10,... | collective-permute-start | bytes 221192 | tf_op jit(solution)/shard_map/ppermute | solution.py:445
  22.0 11.0 %collective-permute-done.1.refs_2_ = f32[144,128]{1,0:T(8,128)S(1)} collective-permute-done((f32[144,128]{1,0:T(8,128)S(1)}, f32[144,128]{1,0:T(8,128)S(1)}, u32[]{:S(2)}, u32[]{:S(2)}) %collective-permute-start.1) | collective-permute-done | bytes 73760 | tf_op jit(solution)/shard_map/ppermute | solution.py:445
  32.9 0.0 collective-permute-start.6
  33.0 4.8 %collective-permute-done.2.refs_3_ = f32[144,128]{1,0:T(8,128)S(1)} collective-permute-done((f32[144,128]{1,0:T(8,128)S(1)}, f32[144,128]{1,0:T(8,128)S(1)}, u32[]{:S(2)}, u32[]{:S(2)}) %collective-permute-start.2) | collective-permute-done | bytes 73760 | tf_op jit(solution)/shard_map/ppermute | solution.py:445
  37.8 0.0 collective-permute-start.7
  37.8 0.0 collective-permute-done.3.refs_0_
  37.8 0.2 collective-permute-start.8
  38.0 0.0 collective-permute-done.4.refs_1_
  38.0 1.0 %collective-permute-start.9 = (f32[144,128]{1,0:T(8,128)S(1)}, f32[144,128]{1,0:T(8,128)S(1)}, u32[]{:S(2)}, u32[]{:S(2)}) collective-permute-start(f32[144,128]{1,0:T(8,128)S(1)} %get-tuple-element.42), channel_id=1, source_target_pairs={{0,10},{1,11},{2,8},{3,9},{4,14},{5,15},{6,12},{7,13},{8,2},{9,3},... | collective-permute-start | bytes 221192 | tf_op jit(solution)/shard_map/ppermute | solution.py:445
  39.0 0.0 collective-permute-done.5.refs_2_
  39.0 3.2 %collective-permute-start.10 = (f32[144,128]{1,0:T(8,128)}, f32[144,128]{1,0:T(8,128)S(1)}, u32[]{:S(2)}, u32[]{:S(2)}) collective-permute-start(f32[144,128]{1,0:T(8,128)} %get-tuple-element.43), channel_id=1, source_target_pairs={{0,11},{1,10},{2,9},{3,8},{4,15},{5,14},{6,13},{7,12},{8,3},{9,2},... | collective-permute-start | bytes 221192 | tf_op jit(solution)/shard_map/ppermute | solution.py:445
  42.2 0.0 collective-permute-done.6.refs_3_
  42.2 0.0 collective-permute-start.11
  42.2 12.1 %collective-permute-done.7.refs_0_ = f32[144,128]{1,0:T(8,128)S(1)} collective-permute-done((f32[144,128]{1,0:T(8,128)S(1)}, f32[144,128]{1,0:T(8,128)S(1)}, u32[]{:S(2)}, u32[]{:S(2)}) %collective-permute-start.7) | collective-permute-done | bytes 73760 | tf_op jit(solution)/shard_map/ppermute | solution.py:445
  54.3 3.9 %collective-permute-start.12 = (f32[144,128]{1,0:T(8,128)}, f32[144,128]{1,0:T(8,128)S(1)}, u32[]{:S(2)}, u32[]{:S(2)}) collective-permute-start(f32[144,128]{1,0:T(8,128)} %get-tuple-element.45), channel_id=1, source_target_pairs={{0,13},{1,12},{2,15},{3,14},{4,9},{5,8},{6,11},{7,10},{8,5},{9,4},... | collective-permute-start | bytes 221192 | tf_op jit(solution)/shard_map/ppermute | solution.py:445
  58.2 0.0 collective-permute-done.8.refs_1_
  58.2 2.2 %collective-permute-start.13 = (f32[144,128]{1,0:T(8,128)}, f32[144,128]{1,0:T(8,128)}, u32[]{:S(2)}, u32[]{:S(2)}) collective-permute-start(f32[144,128]{1,0:T(8,128)} %get-tuple-element.46), channel_id=1, source_target_pairs={{0,14},{1,15},{2,12},{3,13},{4,10},{5,11},{6,8},{7,9},{8,6},{9,7},... | collective-permute-start | bytes 221192 | tf_op jit(solution)/shard_map/ppermute | solution.py:445
  60.4 0.0 collective-permute-done.9.refs_2_
  60.4 2.7 %collective-permute-start.14 = (f32[144,128]{1,0:T(8,128)}, f32[144,128]{1,0:T(8,128)}, u32[]{:S(2)}, u32[]{:S(2)}) collective-permute-start(f32[144,128]{1,0:T(8,128)} %get-tuple-element.47), channel_id=1, source_target_pairs={{0,15},{1,14},{2,13},{3,12},{4,11},{5,10},{6,9},{7,8},{8,7},{9,6},... | collective-permute-start | bytes 221192 | tf_op jit(solution)/shard_map/ppermute | solution.py:445
  63.1 5.5 %all-to-all-done.slots_ref = f32[32,152,128]{2,1,0:T(8,128)S(1)} async-done(((f32[32,152,128]{2,1,0:T(8,128)}), f32[32,152,128]{2,1,0:T(8,128)S(1)}, u32[]{:S(2)}, u32[]{:S(2)}) %all-to-all-start) | async-done | bytes 2490400 | tf_op jit(solution)/shard_map/all_to_all | solution.py:433
  68.6 2.8 %shard_map.69 = (f32[3,8,128]{2,1,0:T(8,128)S(1)}, f32[3,8,128]{2,1,0:T(8,128)S(1)}, f32[8,288,128]{2,1,0:T(8,128)S(1)}, f32[8,288,128]{2,1,0:T(8,128)S(1)}, f32...) custom-call(f32[32,152,128]{2,1,0:T(8,128)S(1)} %all-to-all-done.slots_ref), custom_call_target="tpu_custom_call" | custom-call | tf_op jit(solution)/shard_map/pallas_call | solution.py:450
  71.4 0.0 collective-permute-done.10.refs_3_
  71.4 1.5 %collective-permute-start.15 = (f32[3,8,128]{2,1,0:T(8,128)S(1)}, f32[3,8,128]{2,1,0:T(8,128)S(1)}, u32[]{:S(2)}, u32[]{:S(2)}) collective-permute-start(f32[3,8,128]{2,1,0:T(8,128)S(1)} %get-tuple-element.48), channel_id=1, source_target_pairs={{0,16},{1,17},{2,18},{3,19},{4,20},{5,21},{6,22},{7,23},{8,24},{9,... | collective-permute-start | bytes 36872 | tf_op jit(solution)/shard_map/ppermute | solution.py:455
  72.9 0.1 shard_map.71.refs_0_
  73.0 0.1 shard_map.72.refs_1_
  73.2 0.1 shard_map.73.refs_2_
  73.3 0.0 collective-permute-done.11.refs_0_
  73.3 0.0 collective-permute-done.12.refs_1_
  73.3 0.0 collective-permute-done.13.refs_2_
  73.3 0.0 collective-permute-done.14.refs_3_
  73.4 1.1 %shard_map.74.refs_3_ = f32[2,288,128]{2,1,0:T(8,128)S(1)} custom-call(f32[144,128]{1,0:T(8,128)S(1)} %collective-permute-done.11.refs_0_, f32[144,128]{1,0:T(8,128)S(1)} %collective-permute-done.12.refs_1_, f32[144,128]{1,0:T(8,128)} %collective-permute-done.13.refs_2_, f32[144,128]{1,0:T(8,128)} %collective-permute-done.14.refs_3_), custom_call_target="tpu_custom_call" | custom-call | tf_op jit(solution)/shard_map/pallas_call | solution.py:447
  74.4 0.8 collective-permute-done.15.vector_ref
  75.2 0.1 shard_map.76
  75.4 1.1 %collective-permute-start.16 = (f32[3,8,128]{2,1,0:T(8,128)S(1)}, f32[3,8,128]{2,1,0:T(8,128)S(1)}, u32[]{:S(2)}, u32[]{:S(2)}) collective-permute-start(f32[3,8,128]{2,1,0:T(8,128)S(1)} %shard_map.76), channel_id=1, source_target_pairs={{0,16},{1,17},{2,18},{3,19},{4,20},{5,21},{6,22},{7,23},{8,24},{9,... | collective-permute-start | bytes 36872 | tf_op jit(solution)/shard_map/ppermute | solution.py:455
  76.5 0.1 shard_map.75.own_ref
  76.6 2.2 %collective-permute-done.16.other_ref = f32[3,8,128]{2,1,0:T(8,128)S(1)} collective-permute-done((f32[3,8,128]{2,1,0:T(8,128)S(1)}, f32[3,8,128]{2,1,0:T(8,128)S(1)}, u32[]{:S(2)}, u32[]{:S(2)}) %collective-permute-start.16) | collective-permute-done | bytes 12320 | tf_op jit(solution)/shard_map/ppermute | solution.py:455
  78.9 2.8 %shard_map.77 = f32[128,128]{1,0:T(8,128)S(1)} custom-call(f32[3,8,128]{2,1,0:T(8,128)S(1)} %shard_map.75.own_ref, f32[3,8,128]{2,1,0:T(8,128)S(1)} %collective-permute-done.16.other_ref, f32[8,288,128]{2,1,0:T(8,128)S(1)} %get-tuple-element.49.forward_ref, f32[8,288,128]{2,1,0:T(8,128)S(1)} %get-tuple-element.50.backward_ref, ...), custom_call_target="tpu_custom_call" | custom-call | tf_op jit(solution)/shard_map/pallas_call | solution.py:461
  81.7 13.0 %all_to_all.10 = f32[32,4,128]{2,1,0:T(4,128)S(1)} all-to-all(f32[32,4,128]{2,1,0:T(4,128)S(1)} %bitcast.13), channel_id=1, replica_groups={{0,8,16,24,1,9,17,25,4,12,20,28,5,13,21,29,2,10,18,26,3,11,19,27,6,14,2..., dimensions={0} | all-to-all | bytes 131072 | tf_op jit(solution)/shard_map/all_to_all | solution.py:402
  94.7 1.0 %shard_map.78 = (f32[48,128]{1,0:T(8,128)}, f32[48,128]{1,0:T(8,128)}) custom-call(f32[128,128]{1,0:T(8,128)S(1)} %bitcast.14), custom_call_target="tpu_custom_call" | custom-call | tf_op jit(solution)/shard_map/pallas_call | solution.py:465
Async XLA Ops:
  4.5 64.0 %all-to-all-start = ((f32[32,152,128]{2,1,0:T(8,128)}), f32[32,152,128]{2,1,0:T(8,128)S(1)}, u32[]{:S(2)}, u32[]{:S(2)}) async-start(f32[32,152,128]{2,1,0:T(8,128)} %shard_map.68), calls=%async_computation | async-start | bytes 4980736 | tf_op jit(solution)/shard_map/all_to_all | solution.py:433
  15.8 3.9 %collective-permute-start = (f32[144,128]{1,0:T(8,128)S(1)}, f32[144,128]{1,0:T(8,128)S(1)}, u32[]{:S(2)}, u32[]{:S(2)}) collective-permute-start(f32[144,128]{1,0:T(8,128)S(1)} %get-tuple-element.33), channel_id=1, source_target_pairs={{0,1},{1,0},{2,3},{3,2},{4,5},{5,4},{6,7},{7,6},{8,9},{9,8},{10,11... | collective-permute-start | bytes 221192 | tf_op jit(solution)/shard_map/ppermute | solution.py:445
  16.1 16.8 %collective-permute-start.1 = (f32[144,128]{1,0:T(8,128)S(1)}, f32[144,128]{1,0:T(8,128)S(1)}, u32[]{:S(2)}, u32[]{:S(2)}) collective-permute-start(f32[144,128]{1,0:T(8,128)S(1)} %get-tuple-element.34), channel_id=1, source_target_pairs={{0,2},{1,3},{2,0},{3,1},{4,6},{5,7},{6,4},{7,5},{8,10},{9,11},{10,... | collective-permute-start | bytes 221192 | tf_op jit(solution)/shard_map/ppermute | solution.py:445
  17.6 20.2 %collective-permute-start.2 = (f32[144,128]{1,0:T(8,128)S(1)}, f32[144,128]{1,0:T(8,128)S(1)}, u32[]{:S(2)}, u32[]{:S(2)}) collective-permute-start(f32[144,128]{1,0:T(8,128)S(1)} %get-tuple-element.35), channel_id=1, source_target_pairs={{0,3},{1,2},{2,1},{3,0},{4,7},{5,6},{6,5},{7,4},{8,11},{9,10},{10,... | collective-permute-start | bytes 221192 | tf_op jit(solution)/shard_map/ppermute | solution.py:445
  18.0 19.8 %collective-permute-start.3 = (f32[144,128]{1,0:T(8,128)S(1)}, f32[144,128]{1,0:T(8,128)S(1)}, u32[]{:S(2)}, u32[]{:S(2)}) collective-permute-start(f32[144,128]{1,0:T(8,128)S(1)} %get-tuple-element.36), channel_id=1, source_target_pairs={{0,4},{1,5},{2,6},{3,7},{4,0},{5,1},{6,2},{7,3},{8,12},{9,13},{10,... | collective-permute-start | bytes 221192 | tf_op jit(solution)/shard_map/ppermute | solution.py:445
  19.4 18.6 %collective-permute-start.4 = (f32[144,128]{1,0:T(8,128)S(1)}, f32[144,128]{1,0:T(8,128)S(1)}, u32[]{:S(2)}, u32[]{:S(2)}) collective-permute-start(f32[144,128]{1,0:T(8,128)S(1)} %get-tuple-element.37), channel_id=1, source_target_pairs={{0,5},{1,4},{2,7},{3,6},{4,1},{5,0},{6,3},{7,2},{8,13},{9,12},{10,... | collective-permute-start | bytes 221192 | tf_op jit(solution)/shard_map/ppermute | solution.py:445
  19.7 19.3 %collective-permute-start.5 = (f32[144,128]{1,0:T(8,128)S(1)}, f32[144,128]{1,0:T(8,128)S(1)}, u32[]{:S(2)}, u32[]{:S(2)}) collective-permute-start(f32[144,128]{1,0:T(8,128)S(1)} %get-tuple-element.38), channel_id=1, source_target_pairs={{0,6},{1,7},{2,4},{3,5},{4,2},{5,3},{6,0},{7,1},{8,14},{9,15},{10,... | collective-permute-start | bytes 221192 | tf_op jit(solution)/shard_map/ppermute | solution.py:445
  32.9 9.2 %collective-permute-start.6 = (f32[144,128]{1,0:T(8,128)S(1)}, f32[144,128]{1,0:T(8,128)S(1)}, u32[]{:S(2)}, u32[]{:S(2)}) collective-permute-start(f32[144,128]{1,0:T(8,128)S(1)} %get-tuple-element.39), channel_id=1, source_target_pairs={{0,7},{1,6},{2,5},{3,4},{4,3},{5,2},{6,1},{7,0},{8,15},{9,14},{10,... | collective-permute-start | bytes 221192 | tf_op jit(solution)/shard_map/ppermute | solution.py:445
  37.8 16.6 %collective-permute-start.7 = (f32[144,128]{1,0:T(8,128)S(1)}, f32[144,128]{1,0:T(8,128)S(1)}, u32[]{:S(2)}, u32[]{:S(2)}) collective-permute-start(f32[144,128]{1,0:T(8,128)S(1)} %get-tuple-element.40), channel_id=1, source_target_pairs={{0,8},{1,9},{2,10},{3,11},{4,12},{5,13},{6,14},{7,15},{8,0},{9,1},... | collective-permute-start | bytes 221192 | tf_op jit(solution)/shard_map/ppermute | solution.py:445
  37.8 20.4 %collective-permute-start.8 = (f32[144,128]{1,0:T(8,128)S(1)}, f32[144,128]{1,0:T(8,128)S(1)}, u32[]{:S(2)}, u32[]{:S(2)}) collective-permute-start(f32[144,128]{1,0:T(8,128)S(1)} %get-tuple-element.41), channel_id=1, source_target_pairs={{0,9},{1,8},{2,11},{3,10},{4,13},{5,12},{6,15},{7,14},{8,1},{9,0},... | collective-permute-start | bytes 221192 | tf_op jit(solution)/shard_map/ppermute | solution.py:445
  38.0 22.4 %collective-permute-start.9 = (f32[144,128]{1,0:T(8,128)S(1)}, f32[144,128]{1,0:T(8,128)S(1)}, u32[]{:S(2)}, u32[]{:S(2)}) collective-permute-start(f32[144,128]{1,0:T(8,128)S(1)} %get-tuple-element.42), channel_id=1, source_target_pairs={{0,10},{1,11},{2,8},{3,9},{4,14},{5,15},{6,12},{7,13},{8,2},{9,3},... | collective-permute-start | bytes 221192 | tf_op jit(solution)/shard_map/ppermute | solution.py:445
  39.0 32.4 %collective-permute-start.10 = (f32[144,128]{1,0:T(8,128)}, f32[144,128]{1,0:T(8,128)S(1)}, u32[]{:S(2)}, u32[]{:S(2)}) collective-permute-start(f32[144,128]{1,0:T(8,128)} %get-tuple-element.43), channel_id=1, source_target_pairs={{0,11},{1,10},{2,9},{3,8},{4,15},{5,14},{6,13},{7,12},{8,3},{9,2},... | collective-permute-start | bytes 221192 | tf_op jit(solution)/shard_map/ppermute | solution.py:445
  42.2 31.2 %collective-permute-start.11 = (f32[144,128]{1,0:T(8,128)}, f32[144,128]{1,0:T(8,128)S(1)}, u32[]{:S(2)}, u32[]{:S(2)}) collective-permute-start(f32[144,128]{1,0:T(8,128)} %get-tuple-element.44), channel_id=1, source_target_pairs={{0,12},{1,13},{2,14},{3,15},{4,8},{5,9},{6,10},{7,11},{8,4},{9,5},... | collective-permute-start | bytes 221192 | tf_op jit(solution)/shard_map/ppermute | solution.py:445
  54.3 19.0 %collective-permute-start.12 = (f32[144,128]{1,0:T(8,128)}, f32[144,128]{1,0:T(8,128)S(1)}, u32[]{:S(2)}, u32[]{:S(2)}) collective-permute-start(f32[144,128]{1,0:T(8,128)} %get-tuple-element.45), channel_id=1, source_target_pairs={{0,13},{1,12},{2,15},{3,14},{4,9},{5,8},{6,11},{7,10},{8,5},{9,4},... | collective-permute-start | bytes 221192 | tf_op jit(solution)/shard_map/ppermute | solution.py:445
  58.2 15.2 %collective-permute-start.13 = (f32[144,128]{1,0:T(8,128)}, f32[144,128]{1,0:T(8,128)}, u32[]{:S(2)}, u32[]{:S(2)}) collective-permute-start(f32[144,128]{1,0:T(8,128)} %get-tuple-element.46), channel_id=1, source_target_pairs={{0,14},{1,15},{2,12},{3,13},{4,10},{5,11},{6,8},{7,9},{8,6},{9,7},... | collective-permute-start | bytes 221192 | tf_op jit(solution)/shard_map/ppermute | solution.py:445
  60.4 12.9 %collective-permute-start.14 = (f32[144,128]{1,0:T(8,128)}, f32[144,128]{1,0:T(8,128)}, u32[]{:S(2)}, u32[]{:S(2)}) collective-permute-start(f32[144,128]{1,0:T(8,128)} %get-tuple-element.47), channel_id=1, source_target_pairs={{0,15},{1,14},{2,13},{3,12},{4,11},{5,10},{6,9},{7,8},{8,7},{9,6},... | collective-permute-start | bytes 221192 | tf_op jit(solution)/shard_map/ppermute | solution.py:445
  71.4 3.8 %collective-permute-start.15 = (f32[3,8,128]{2,1,0:T(8,128)S(1)}, f32[3,8,128]{2,1,0:T(8,128)S(1)}, u32[]{:S(2)}, u32[]{:S(2)}) collective-permute-start(f32[3,8,128]{2,1,0:T(8,128)S(1)} %get-tuple-element.48), channel_id=1, source_target_pairs={{0,16},{1,17},{2,18},{3,19},{4,20},{5,21},{6,22},{7,23},{8,24},{9,... | collective-permute-start | bytes 36872 | tf_op jit(solution)/shard_map/ppermute | solution.py:455
  75.4 3.5 %collective-permute-start.16 = (f32[3,8,128]{2,1,0:T(8,128)S(1)}, f32[3,8,128]{2,1,0:T(8,128)S(1)}, u32[]{:S(2)}, u32[]{:S(2)}) collective-permute-start(f32[3,8,128]{2,1,0:T(8,128)S(1)} %shard_map.76), channel_id=1, source_target_pairs={{0,16},{1,17},{2,18},{3,19},{4,20},{5,21},{6,22},{7,23},{8,24},{9,... | collective-permute-start | bytes 36872 | tf_op jit(solution)/shard_map/ppermute | solution.py:455

commit v3 on v2

--- a/solution.py
+++ b/solution.py
@@ -13,7 +13,7 @@
 
 
 def chunk_of(cell, station):
-    return 16 * (station // 2) + 8 * (cell % 2) + 4 * (station % 2) + cell // 2
+    return 16 * (cell % 2) + 8 * (station % 2) + 4 * (station // 2) + cell // 2
 
 
 ORDER = [[e for chunk in range(32) for e in range(32) if chunk_of(e // 4, e % 4) == chunk]]

time: 96.8 us -> 97.1 us (level)
  starting transfers between devices: 29 us -> 31.1 us
  waiting for transfers between devices: 36.5 us -> 35.2 us
    ppermute x2, starting transfers between devices: 2.6 us -> 5.42 us  [with_partner(): return lax.ppermute(vector, BOTH, [(e, e ^ 16) for e in range(32)])]
    ppermute x2, waiting for transfers between devices: 3.06 us -> 1.46 us  [with_partner(): return lax.ppermute(vector, BOTH, [(e, e ^ 16) for e in range(32)])]
  transfers between devices with their start and end apart: 18 -> 18, of which waited for: 6 -> 8; matrix products, arithmetic and copies ran while one was open for 0% -> 0% of each run, Pallas kernels for 9% -> 9%
where the time goes in v3:
time: 97.1 us; the launch traced here: 96.5 us
  waiting for transfers between devices  35.2 us (36%)
  starting transfers between devices  31.1 us (32%)
  Pallas kernels  16.4 us (17%)
  blocking collectives  13.1 us (13%)
    ppermute x15, waiting for transfers between devices, line_plan(): lax.ppermute(parts[d], BOTH, [(e, e ^ d) for e in range(32)])  28.2 us
    ppermute x15, starting transfers between devices, line_plan(): lax.ppermute(parts[d], BOTH, [(e, e ^ d) for e in range(32)])  18.6 us
    all_to_all x1, blocking collectives, exchange(): lax.all_to_all(slots.reshape(32, rows, 128), BOTH, 0, 0, axis_index_group...  13.1 us
    all_to_all x1, starting transfers between devices, line_plan(): lax.all_to_all(slots, BOTH, 0, 0, axis_index_groups=ORDER, tiled=True)  7.1 us
    all_to_all x1, waiting for transfers between devices, line_plan(): lax.all_to_all(slots, BOTH, 0, 0, axis_index_groups=ORDER, tiled=True)  5.47 us
    ppermute x2, starting transfers between devices, with_partner(): return lax.ppermute(vector, BOTH, [(e, e ^ 16) for e in range(32)])  5.42 us
    pallas_call x1, Pallas kernels, line_plan(): pl.pallas_call(inverse_send_kernel, out_shape=[shaped(144, 128)] * 16, in...  4.14 us
    pallas_call x1, Pallas kernels, line_plan(): pl.pallas_call(first_send_kernel, out_shape=pltpu.HBM((32, 152, 128), f32...  3.89 us
  transfers between devices with their start and end apart: 18, of which 8 were waited for; matrix products, arithmetic and copies ran while one was open for 0% of the time, Pallas kernels for 9%

profile of v3, /device:TPU:1, one launch (start us, length us, event | category | flops | bytes accessed | tf_op | source)
XLA Modules:
  0.0 96.5 jit_solution(5609486534260829273)
XLA Ops:
  0.6 3.9 %shard_map.68 = f32[32,152,128]{2,1,0:T(8,128)} custom-call(bf16[48,48,128]{2,1,0:T(8,128)(2,1)} %bitcast.17, bf16[48,48,128]{2,1,0:T(8,128)(2,1)} %bitcast.18, bf16[48,48,128]{2,1,0:T(8,128)(2,1)} %bitcast.15, f32[48,128]{1,0:T(8,128)} %bitcast.19, f32[48,128]{1,0:T(8,128)} %bitcast.20), custom_call_target="tpu_custom_call" | custom-call | tf_op jit(solution)/shard_map/pallas_call | solution.py:415
  4.5 7.1 %all-to-all-start = ((f32[32,152,128]{2,1,0:T(8,128)}), f32[32,152,128]{2,1,0:T(8,128)S(1)}, u32[]{:S(2)}, u32[]{:S(2)}) async-start(f32[32,152,128]{2,1,0:T(8,128)} %shard_map.68), calls=%async_computation | async-start | bytes 4980736 | tf_op jit(solution)/shard_map/all_to_all | solution.py:433
  11.6 4.1 %shard_map.70 = (f32[144,128]{1,0:T(8,128)S(1)}, f32[144,128]{1,0:T(8,128)S(1)}, f32[144,128]{1,0:T(8,128)S(1)}, f32[144,128]{1,0:T(8,128)S(1)}, f32[144,128]{1,...) custom-call(bf16[48,48,128]{2,1,0:T(8,128)(2,1)} %bitcast.16), custom_call_target="tpu_custom_call" | custom-call | tf_op jit(solution)/shard_map/pallas_call | solution.py:435
  15.8 0.3 collective-permute-start
  16.1 1.5 %collective-permute-start.1 = (f32[144,128]{1,0:T(8,128)S(1)}, f32[144,128]{1,0:T(8,128)S(1)}, u32[]{:S(2)}, u32[]{:S(2)}) collective-permute-start(f32[144,128]{1,0:T(8,128)S(1)} %get-tuple-element.34), channel_id=1, source_target_pairs={{0,2},{1,3},{2,0},{3,1},{4,6},{5,7},{6,4},{7,5},{8,10},{9,11},{10,... | collective-permute-start | bytes 221192 | tf_op jit(solution)/shard_map/ppermute | solution.py:445
  17.6 0.4 collective-permute-start.2
  18.0 1.4 %collective-permute-start.3 = (f32[144,128]{1,0:T(8,128)S(1)}, f32[144,128]{1,0:T(8,128)S(1)}, u32[]{:S(2)}, u32[]{:S(2)}) collective-permute-start(f32[144,128]{1,0:T(8,128)S(1)} %get-tuple-element.36), channel_id=1, source_target_pairs={{0,4},{1,5},{2,6},{3,7},{4,0},{5,1},{6,2},{7,3},{8,12},{9,13},{10,... | collective-permute-start | bytes 221192 | tf_op jit(solution)/shard_map/ppermute | solution.py:445
  19.4 0.3 collective-permute-start.4
  19.7 0.0 collective-permute-done.refs_1_
  19.7 2.3 %collective-permute-start.5 = (f32[144,128]{1,0:T(8,128)S(1)}, f32[144,128]{1,0:T(8,128)S(1)}, u32[]{:S(2)}, u32[]{:S(2)}) collective-permute-start(f32[144,128]{1,0:T(8,128)S(1)} %get-tuple-element.38), channel_id=1, source_target_pairs={{0,6},{1,7},{2,4},{3,5},{4,2},{5,3},{6,0},{7,1},{8,14},{9,15},{10,... | collective-permute-start | bytes 221192 | tf_op jit(solution)/shard_map/ppermute | solution.py:445
  22.0 6.8 %collective-permute-done.1.refs_2_ = f32[144,128]{1,0:T(8,128)S(1)} collective-permute-done((f32[144,128]{1,0:T(8,128)S(1)}, f32[144,128]{1,0:T(8,128)S(1)}, u32[]{:S(2)}, u32[]{:S(2)}) %collective-permute-start.1) | collective-permute-done | bytes 73760 | tf_op jit(solution)/shard_map/ppermute | solution.py:445
  28.8 2.2 %collective-permute-start.6 = (f32[144,128]{1,0:T(8,128)S(1)}, f32[144,128]{1,0:T(8,128)S(1)}, u32[]{:S(2)}, u32[]{:S(2)}) collective-permute-start(f32[144,128]{1,0:T(8,128)S(1)} %get-tuple-element.39), channel_id=1, source_target_pairs={{0,7},{1,6},{2,5},{3,4},{4,3},{5,2},{6,1},{7,0},{8,15},{9,14},{10,... | collective-permute-start | bytes 221192 | tf_op jit(solution)/shard_map/ppermute | solution.py:445
  31.0 2.0 %collective-permute-done.2.refs_3_ = f32[144,128]{1,0:T(8,128)S(1)} collective-permute-done((f32[144,128]{1,0:T(8,128)S(1)}, f32[144,128]{1,0:T(8,128)S(1)}, u32[]{:S(2)}, u32[]{:S(2)}) %collective-permute-start.2) | collective-permute-done | bytes 73760 | tf_op jit(solution)/shard_map/ppermute | solution.py:445
  33.0 0.0 collective-permute-start.7
  33.0 0.0 collective-permute-done.3.refs_0_
  33.0 1.2 %collective-permute-start.8 = (f32[144,128]{1,0:T(8,128)S(1)}, f32[144,128]{1,0:T(8,128)S(1)}, u32[]{:S(2)}, u32[]{:S(2)}) collective-permute-start(f32[144,128]{1,0:T(8,128)S(1)} %get-tuple-element.41), channel_id=1, source_target_pairs={{0,9},{1,8},{2,11},{3,10},{4,13},{5,12},{6,15},{7,14},{8,1},{9,0},... | collective-permute-start | bytes 221192 | tf_op jit(solution)/shard_map/ppermute | solution.py:445
  34.2 1.6 %collective-permute-done.4.refs_1_ = f32[144,128]{1,0:T(8,128)S(1)} collective-permute-done((f32[144,128]{1,0:T(8,128)S(1)}, f32[144,128]{1,0:T(8,128)S(1)}, u32[]{:S(2)}, u32[]{:S(2)}) %collective-permute-start.4) | collective-permute-done | bytes 73760 | tf_op jit(solution)/shard_map/ppermute | solution.py:445
  35.8 0.0 collective-permute-start.9
  35.8 2.0 %collective-permute-done.5.refs_2_ = f32[144,128]{1,0:T(8,128)S(1)} collective-permute-done((f32[144,128]{1,0:T(8,128)S(1)}, f32[144,128]{1,0:T(8,128)S(1)}, u32[]{:S(2)}, u32[]{:S(2)}) %collective-permute-start.5) | collective-permute-done | bytes 73760 | tf_op jit(solution)/shard_map/ppermute | solution.py:445
  37.8 1.4 %collective-permute-start.10 = (f32[144,128]{1,0:T(8,128)}, f32[144,128]{1,0:T(8,128)S(1)}, u32[]{:S(2)}, u32[]{:S(2)}) collective-permute-start(f32[144,128]{1,0:T(8,128)} %get-tuple-element.43), channel_id=1, source_target_pairs={{0,11},{1,10},{2,9},{3,8},{4,15},{5,14},{6,13},{7,12},{8,3},{9,2},... | collective-permute-start | bytes 221192 | tf_op jit(solution)/shard_map/ppermute | solution.py:445
  39.2 2.6 %collective-permute-done.6.refs_3_ = f32[144,128]{1,0:T(8,128)S(1)} collective-permute-done((f32[144,128]{1,0:T(8,128)S(1)}, f32[144,128]{1,0:T(8,128)S(1)}, u32[]{:S(2)}, u32[]{:S(2)}) %collective-permute-start.6) | collective-permute-done | bytes 73760 | tf_op jit(solution)/shard_map/ppermute | solution.py:445
  41.8 0.0 collective-permute-start.11
  41.8 13.2 %collective-permute-done.7.refs_0_ = f32[144,128]{1,0:T(8,128)S(1)} collective-permute-done((f32[144,128]{1,0:T(8,128)S(1)}, f32[144,128]{1,0:T(8,128)S(1)}, u32[]{:S(2)}, u32[]{:S(2)}) %collective-permute-start.7) | collective-permute-done | bytes 73760 | tf_op jit(solution)/shard_map/ppermute | solution.py:445
  55.0 3.5 %collective-permute-start.12 = (f32[144,128]{1,0:T(8,128)}, f32[144,128]{1,0:T(8,128)S(1)}, u32[]{:S(2)}, u32[]{:S(2)}) collective-permute-start(f32[144,128]{1,0:T(8,128)} %get-tuple-element.45), channel_id=1, source_target_pairs={{0,13},{1,12},{2,15},{3,14},{4,9},{5,8},{6,11},{7,10},{8,5},{9,4},... | collective-permute-start | bytes 221192 | tf_op jit(solution)/shard_map/ppermute | solution.py:445
  58.5 0.0 collective-permute-done.8.refs_1_
  58.5 2.0 %collective-permute-start.13 = (f32[144,128]{1,0:T(8,128)}, f32[144,128]{1,0:T(8,128)}, u32[]{:S(2)}, u32[]{:S(2)}) collective-permute-start(f32[144,128]{1,0:T(8,128)} %get-tuple-element.46), channel_id=1, source_target_pairs={{0,14},{1,15},{2,12},{3,13},{4,10},{5,11},{6,8},{7,9},{8,6},{9,7},... | collective-permute-start | bytes 221192 | tf_op jit(solution)/shard_map/ppermute | solution.py:445
  60.6 0.0 collective-permute-done.9.refs_2_
  60.6 2.0 %collective-permute-start.14 = (f32[144,128]{1,0:T(8,128)}, f32[144,128]{1,0:T(8,128)}, u32[]{:S(2)}, u32[]{:S(2)}) collective-permute-start(f32[144,128]{1,0:T(8,128)} %get-tuple-element.47), channel_id=1, source_target_pairs={{0,15},{1,14},{2,13},{3,12},{4,11},{5,10},{6,9},{7,8},{8,7},{9,6},... | collective-permute-start | bytes 221192 | tf_op jit(solution)/shard_map/ppermute | solution.py:445
  62.6 5.5 %all-to-all-done.slots_ref = f32[32,152,128]{2,1,0:T(8,128)S(1)} async-done(((f32[32,152,128]{2,1,0:T(8,128)}), f32[32,152,128]{2,1,0:T(8,128)S(1)}, u32[]{:S(2)}, u32[]{:S(2)}) %all-to-all-start) | async-done | bytes 2490400 | tf_op jit(solution)/shard_map/all_to_all | solution.py:433
  68.1 2.8 %shard_map.69 = (f32[3,8,128]{2,1,0:T(8,128)S(1)}, f32[3,8,128]{2,1,0:T(8,128)S(1)}, f32[8,288,128]{2,1,0:T(8,128)S(1)}, f32[8,288,128]{2,1,0:T(8,128)S(1)}, f32...) custom-call(f32[32,152,128]{2,1,0:T(8,128)S(1)} %all-to-all-done.slots_ref), custom_call_target="tpu_custom_call" | custom-call | tf_op jit(solution)/shard_map/pallas_call | solution.py:450
  70.9 0.0 collective-permute-done.10.refs_3_
  70.9 3.5 %collective-permute-start.15 = (f32[3,8,128]{2,1,0:T(8,128)S(1)}, f32[3,8,128]{2,1,0:T(8,128)S(1)}, u32[]{:S(2)}, u32[]{:S(2)}) collective-permute-start(f32[3,8,128]{2,1,0:T(8,128)S(1)} %get-tuple-element.48), channel_id=1, source_target_pairs={{0,16},{1,17},{2,18},{3,19},{4,20},{5,21},{6,22},{7,23},{8,24},{9,... | collective-permute-start | bytes 36872 | tf_op jit(solution)/shard_map/ppermute | solution.py:455
  74.4 0.1 shard_map.71.refs_0_
  74.5 0.1 shard_map.72.refs_1_
  74.7 0.1 shard_map.73.refs_2_
  74.8 0.0 collective-permute-done.11.refs_0_
  74.8 0.0 collective-permute-done.12.refs_1_
  74.9 0.0 collective-permute-done.13.refs_2_
  74.9 0.0 collective-permute-done.14.refs_3_
  74.9 1.1 %shard_map.74.refs_3_ = f32[2,288,128]{2,1,0:T(8,128)S(1)} custom-call(f32[144,128]{1,0:T(8,128)S(1)} %collective-permute-done.11.refs_0_, f32[144,128]{1,0:T(8,128)S(1)} %collective-permute-done.12.refs_1_, f32[144,128]{1,0:T(8,128)} %collective-permute-done.13.refs_2_, f32[144,128]{1,0:T(8,128)} %collective-permute-done.14.refs_3_), custom_call_target="tpu_custom_call" | custom-call | tf_op jit(solution)/shard_map/pallas_call | solution.py:447
  75.9 0.0 collective-permute-done.15.vector_ref
  76.0 0.1 shard_map.76
  76.1 1.9 %collective-permute-start.16 = (f32[3,8,128]{2,1,0:T(8,128)S(1)}, f32[3,8,128]{2,1,0:T(8,128)S(1)}, u32[]{:S(2)}, u32[]{:S(2)}) collective-permute-start(f32[3,8,128]{2,1,0:T(8,128)S(1)} %shard_map.76), channel_id=1, source_target_pairs={{0,16},{1,17},{2,18},{3,19},{4,20},{5,21},{6,22},{7,23},{8,24},{9,... | collective-permute-start | bytes 36872 | tf_op jit(solution)/shard_map/ppermute | solution.py:455
  78.0 0.1 shard_map.75.own_ref
  78.2 1.5 %collective-permute-done.16.other_ref = f32[3,8,128]{2,1,0:T(8,128)S(1)} collective-permute-done((f32[3,8,128]{2,1,0:T(8,128)S(1)}, f32[3,8,128]{2,1,0:T(8,128)S(1)}, u32[]{:S(2)}, u32[]{:S(2)}) %collective-permute-start.16) | collective-permute-done | bytes 12320 | tf_op jit(solution)/shard_map/ppermute | solution.py:455
  79.6 2.8 %shard_map.77 = f32[128,128]{1,0:T(8,128)S(1)} custom-call(f32[3,8,128]{2,1,0:T(8,128)S(1)} %shard_map.75.own_ref, f32[3,8,128]{2,1,0:T(8,128)S(1)} %collective-permute-done.16.other_ref, f32[8,288,128]{2,1,0:T(8,128)S(1)} %get-tuple-element.49.forward_ref, f32[8,288,128]{2,1,0:T(8,128)S(1)} %get-tuple-element.50.backward_ref, ...), custom_call_target="tpu_custom_call" | custom-call | tf_op jit(solution)/shard_map/pallas_call | solution.py:461
  82.4 13.1 %all_to_all.10 = f32[32,4,128]{2,1,0:T(4,128)S(1)} all-to-all(f32[32,4,128]{2,1,0:T(4,128)S(1)} %bitcast.13), channel_id=1, replica_groups={{0,8,16,24,2,10,18,26,1,9,17,25,3,11,19,27,4,12,20,28,6,14,22,30,5,13,2..., dimensions={0} | all-to-all | bytes 131072 | tf_op jit(solution)/shard_map/all_to_all | solution.py:402
  95.5 1.0 %shard_map.78 = (f32[48,128]{1,0:T(8,128)}, f32[48,128]{1,0:T(8,128)}) custom-call(f32[128,128]{1,0:T(8,128)S(1)} %bitcast.14), custom_call_target="tpu_custom_call" | custom-call | tf_op jit(solution)/shard_map/pallas_call | solution.py:465
Async XLA Ops:
  4.5 63.5 %all-to-all-start = ((f32[32,152,128]{2,1,0:T(8,128)}), f32[32,152,128]{2,1,0:T(8,128)S(1)}, u32[]{:S(2)}, u32[]{:S(2)}) async-start(f32[32,152,128]{2,1,0:T(8,128)} %shard_map.68), calls=%async_computation | async-start | bytes 4980736 | tf_op jit(solution)/shard_map/all_to_all | solution.py:433
  15.8 3.9 %collective-permute-start = (f32[144,128]{1,0:T(8,128)S(1)}, f32[144,128]{1,0:T(8,128)S(1)}, u32[]{:S(2)}, u32[]{:S(2)}) collective-permute-start(f32[144,128]{1,0:T(8,128)S(1)} %get-tuple-element.33), channel_id=1, source_target_pairs={{0,1},{1,0},{2,3},{3,2},{4,5},{5,4},{6,7},{7,6},{8,9},{9,8},{10,11... | collective-permute-start | bytes 221192 | tf_op jit(solution)/shard_map/ppermute | solution.py:445
  16.1 12.7 %collective-permute-start.1 = (f32[144,128]{1,0:T(8,128)S(1)}, f32[144,128]{1,0:T(8,128)S(1)}, u32[]{:S(2)}, u32[]{:S(2)}) collective-permute-start(f32[144,128]{1,0:T(8,128)S(1)} %get-tuple-element.34), channel_id=1, source_target_pairs={{0,2},{1,3},{2,0},{3,1},{4,6},{5,7},{6,4},{7,5},{8,10},{9,11},{10,... | collective-permute-start | bytes 221192 | tf_op jit(solution)/shard_map/ppermute | solution.py:445
  17.6 15.4 %collective-permute-start.2 = (f32[144,128]{1,0:T(8,128)S(1)}, f32[144,128]{1,0:T(8,128)S(1)}, u32[]{:S(2)}, u32[]{:S(2)}) collective-permute-start(f32[144,128]{1,0:T(8,128)S(1)} %get-tuple-element.35), channel_id=1, source_target_pairs={{0,3},{1,2},{2,1},{3,0},{4,7},{5,6},{6,5},{7,4},{8,11},{9,10},{10,... | collective-permute-start | bytes 221192 | tf_op jit(solution)/shard_map/ppermute | solution.py:445
  18.0 15.0 %collective-permute-start.3 = (f32[144,128]{1,0:T(8,128)S(1)}, f32[144,128]{1,0:T(8,128)S(1)}, u32[]{:S(2)}, u32[]{:S(2)}) collective-permute-start(f32[144,128]{1,0:T(8,128)S(1)} %get-tuple-element.36), channel_id=1, source_target_pairs={{0,4},{1,5},{2,6},{3,7},{4,0},{5,1},{6,2},{7,3},{8,12},{9,13},{10,... | collective-permute-start | bytes 221192 | tf_op jit(solution)/shard_map/ppermute | solution.py:445
  19.4 16.4 %collective-permute-start.4 = (f32[144,128]{1,0:T(8,128)S(1)}, f32[144,128]{1,0:T(8,128)S(1)}, u32[]{:S(2)}, u32[]{:S(2)}) collective-permute-start(f32[144,128]{1,0:T(8,128)S(1)} %get-tuple-element.37), channel_id=1, source_target_pairs={{0,5},{1,4},{2,7},{3,6},{4,1},{5,0},{6,3},{7,2},{8,13},{9,12},{10,... | collective-permute-start | bytes 221192 | tf_op jit(solution)/shard_map/ppermute | solution.py:445
  19.7 18.1 %collective-permute-start.5 = (f32[144,128]{1,0:T(8,128)S(1)}, f32[144,128]{1,0:T(8,128)S(1)}, u32[]{:S(2)}, u32[]{:S(2)}) collective-permute-start(f32[144,128]{1,0:T(8,128)S(1)} %get-tuple-element.38), channel_id=1, source_target_pairs={{0,6},{1,7},{2,4},{3,5},{4,2},{5,3},{6,0},{7,1},{8,14},{9,15},{10,... | collective-permute-start | bytes 221192 | tf_op jit(solution)/shard_map/ppermute | solution.py:445
  28.8 13.0 %collective-permute-start.6 = (f32[144,128]{1,0:T(8,128)S(1)}, f32[144,128]{1,0:T(8,128)S(1)}, u32[]{:S(2)}, u32[]{:S(2)}) collective-permute-start(f32[144,128]{1,0:T(8,128)S(1)} %get-tuple-element.39), channel_id=1, source_target_pairs={{0,7},{1,6},{2,5},{3,4},{4,3},{5,2},{6,1},{7,0},{8,15},{9,14},{10,... | collective-permute-start | bytes 221192 | tf_op jit(solution)/shard_map/ppermute | solution.py:445
  33.0 22.0 %collective-permute-start.7 = (f32[144,128]{1,0:T(8,128)S(1)}, f32[144,128]{1,0:T(8,128)S(1)}, u32[]{:S(2)}, u32[]{:S(2)}) collective-permute-start(f32[144,128]{1,0:T(8,128)S(1)} %get-tuple-element.40), channel_id=1, source_target_pairs={{0,8},{1,9},{2,10},{3,11},{4,12},{5,13},{6,14},{7,15},{8,0},{9,1},... | collective-permute-start | bytes 221192 | tf_op jit(solution)/shard_map/ppermute | solution.py:445
  33.0 25.5 %collective-permute-start.8 = (f32[144,128]{1,0:T(8,128)S(1)}, f32[144,128]{1,0:T(8,128)S(1)}, u32[]{:S(2)}, u32[]{:S(2)}) collective-permute-start(f32[144,128]{1,0:T(8,128)S(1)} %get-tuple-element.41), channel_id=1, source_target_pairs={{0,9},{1,8},{2,11},{3,10},{4,13},{5,12},{6,15},{7,14},{8,1},{9,0},... | collective-permute-start | bytes 221192 | tf_op jit(solution)/shard_map/ppermute | solution.py:445
  35.8 24.8 %collective-permute-start.9 = (f32[144,128]{1,0:T(8,128)S(1)}, f32[144,128]{1,0:T(8,128)S(1)}, u32[]{:S(2)}, u32[]{:S(2)}) collective-permute-start(f32[144,128]{1,0:T(8,128)S(1)} %get-tuple-element.42), channel_id=1, source_target_pairs={{0,10},{1,11},{2,8},{3,9},{4,14},{5,15},{6,12},{7,13},{8,2},{9,3},... | collective-permute-start | bytes 221192 | tf_op jit(solution)/shard_map/ppermute | solution.py:445
  37.8 33.1 %collective-permute-start.10 = (f32[144,128]{1,0:T(8,128)}, f32[144,128]{1,0:T(8,128)S(1)}, u32[]{:S(2)}, u32[]{:S(2)}) collective-permute-start(f32[144,128]{1,0:T(8,128)} %get-tuple-element.43), channel_id=1, source_target_pairs={{0,11},{1,10},{2,9},{3,8},{4,15},{5,14},{6,13},{7,12},{8,3},{9,2},... | collective-permute-start | bytes 221192 | tf_op jit(solution)/shard_map/ppermute | solution.py:445
  41.8 33.0 %collective-permute-start.11 = (f32[144,128]{1,0:T(8,128)}, f32[144,128]{1,0:T(8,128)S(1)}, u32[]{:S(2)}, u32[]{:S(2)}) collective-permute-start(f32[144,128]{1,0:T(8,128)} %get-tuple-element.44), channel_id=1, source_target_pairs={{0,12},{1,13},{2,14},{3,15},{4,8},{5,9},{6,10},{7,11},{8,4},{9,5},... | collective-permute-start | bytes 221192 | tf_op jit(solution)/shard_map/ppermute | solution.py:445
  55.0 19.8 %collective-permute-start.12 = (f32[144,128]{1,0:T(8,128)}, f32[144,128]{1,0:T(8,128)S(1)}, u32[]{:S(2)}, u32[]{:S(2)}) collective-permute-start(f32[144,128]{1,0:T(8,128)} %get-tuple-element.45), channel_id=1, source_target_pairs={{0,13},{1,12},{2,15},{3,14},{4,9},{5,8},{6,11},{7,10},{8,5},{9,4},... | collective-permute-start | bytes 221192 | tf_op jit(solution)/shard_map/ppermute | solution.py:445
  58.5 16.3 %collective-permute-start.13 = (f32[144,128]{1,0:T(8,128)}, f32[144,128]{1,0:T(8,128)}, u32[]{:S(2)}, u32[]{:S(2)}) collective-permute-start(f32[144,128]{1,0:T(8,128)} %get-tuple-element.46), channel_id=1, source_target_pairs={{0,14},{1,15},{2,12},{3,13},{4,10},{5,11},{6,8},{7,9},{8,6},{9,7},... | collective-permute-start | bytes 221192 | tf_op jit(solution)/shard_map/ppermute | solution.py:445
  60.6 14.3 %collective-permute-start.14 = (f32[144,128]{1,0:T(8,128)}, f32[144,128]{1,0:T(8,128)}, u32[]{:S(2)}, u32[]{:S(2)}) collective-permute-start(f32[144,128]{1,0:T(8,128)} %get-tuple-element.47), channel_id=1, source_target_pairs={{0,15},{1,14},{2,13},{3,12},{4,11},{5,10},{6,9},{7,8},{8,7},{9,6},... | collective-permute-start | bytes 221192 | tf_op jit(solution)/shard_map/ppermute | solution.py:445
  70.9 5.1 %collective-permute-start.15 = (f32[3,8,128]{2,1,0:T(8,128)S(1)}, f32[3,8,128]{2,1,0:T(8,128)S(1)}, u32[]{:S(2)}, u32[]{:S(2)}) collective-permute-start(f32[3,8,128]{2,1,0:T(8,128)S(1)} %get-tuple-element.48), channel_id=1, source_target_pairs={{0,16},{1,17},{2,18},{3,19},{4,20},{5,21},{6,22},{7,23},{8,24},{9,... | collective-permute-start | bytes 36872 | tf_op jit(solution)/shard_map/ppermute | solution.py:455
  76.1 3.5 %collective-permute-start.16 = (f32[3,8,128]{2,1,0:T(8,128)S(1)}, f32[3,8,128]{2,1,0:T(8,128)S(1)}, u32[]{:S(2)}, u32[]{:S(2)}) collective-permute-start(f32[3,8,128]{2,1,0:T(8,128)S(1)} %shard_map.76), channel_id=1, source_target_pairs={{0,16},{1,17},{2,18},{3,19},{4,20},{5,21},{6,22},{7,23},{8,24},{9,... | collective-permute-start | bytes 36872 | tf_op jit(solution)/shard_map/ppermute | solution.py:455

commit v4 on v3

--- a/solution.py
+++ b/solution.py
@@ -13,7 +13,7 @@
 
 
 def chunk_of(cell, station):
-    return 16 * (cell % 2) + 8 * (station % 2) + 4 * (station // 2) + cell // 2
+    return 16 * (cell % 2) + 4 * station + 3 - cell // 2
 
 
 ORDER = [[e for chunk in range(32) for e in range(32) if chunk_of(e // 4, e % 4) == chunk]]
@@ -39,7 +39,7 @@
 
 
 def line_lanes(other_half=0):
-    return lane_index() + 16 - 4 * ((lax.axis_index("azim") // 2) ^ (2 * other_half))
+    return lane_index() + 16 - 4 * ((3 - lax.axis_index("azim") // 2) ^ (2 * other_half))
 
 
 def own_chunk():

time: 97.1 us -> 96.9 us (level)
  waiting for transfers between devices: 35.2 us -> 31.1 us
  starting transfers between devices: 31.1 us -> 34 us
  blocking collectives: 13.1 us -> 14.2 us
    ppermute x15, starting transfers between devices: 18.6 us -> 25.9 us  [line_plan(): lax.ppermute(parts[d], BOTH, [(e, e ^ d) for e in range(32)])]
    ppermute x15, waiting for transfers between devices: 28.2 us -> 21.3 us  [line_plan(): lax.ppermute(parts[d], BOTH, [(e, e ^ d) for e in range(32)])]
    ppermute x2, starting transfers between devices: 5.42 us -> 0.98 us  [with_partner(): return lax.ppermute(vector, BOTH, [(e, e ^ 16) for e in range(32)])]
    ppermute x2, waiting for transfers between devices: 1.46 us -> 4.35 us  [with_partner(): return lax.ppermute(vector, BOTH, [(e, e ^ 16) for e in range(32)])]
    all_to_all x1, blocking collectives: 13.1 us -> 14.2 us  [exchange(): lax.all_to_all(slots.reshape(32, rows, 128), BOTH, 0, 0, axis_index_group...]
  transfers between devices with their start and end apart: 18 -> 18, of which waited for: 8 -> 7; matrix products, arithmetic and copies ran while one was open for 0% -> 0% of each run, Pallas kernels for 9% -> 9%
where the time goes in v4:
time: 96.9 us; the launch traced here: 96.2 us
  starting transfers between devices  34 us (35%)
  waiting for transfers between devices  31.1 us (32%)
  Pallas kernels  16.3 us (17%)
  blocking collectives  14.2 us (15%)
    ppermute x15, starting transfers between devices, line_plan(): lax.ppermute(parts[d], BOTH, [(e, e ^ d) for e in range(32)])  25.9 us
    ppermute x15, waiting for transfers between devices, line_plan(): lax.ppermute(parts[d], BOTH, [(e, e ^ d) for e in range(32)])  21.3 us
    all_to_all x1, blocking collectives, exchange(): lax.all_to_all(slots.reshape(32, rows, 128), BOTH, 0, 0, axis_index_group...  14.2 us
    all_to_all x1, starting transfers between devices, line_plan(): lax.all_to_all(slots, BOTH, 0, 0, axis_index_groups=ORDER, tiled=True)  7.1 us
    all_to_all x1, waiting for transfers between devices, line_plan(): lax.all_to_all(slots, BOTH, 0, 0, axis_index_groups=ORDER, tiled=True)  5.44 us
    ppermute x2, waiting for transfers between devices, with_partner(): return lax.ppermute(vector, BOTH, [(e, e ^ 16) for e in range(32)])  4.35 us
    pallas_call x1, Pallas kernels, line_plan(): pl.pallas_call(inverse_send_kernel, out_shape=[shaped(144, 128)] * 16, in...  4.07 us
    pallas_call x1, Pallas kernels, line_plan(): pl.pallas_call(first_send_kernel, out_shape=pltpu.HBM((32, 152, 128), f32...  3.89 us
  transfers between devices with their start and end apart: 18, of which 7 were waited for; matrix products, arithmetic and copies ran while one was open for 0% of the time, Pallas kernels for 9%

profile of v4, /device:TPU:1, one launch (start us, length us, event | category | flops | bytes accessed | tf_op | source)
XLA Modules:
  0.0 96.2 jit_solution(3350474599437627318)
XLA Ops:
  0.6 3.9 %shard_map.68 = f32[32,152,128]{2,1,0:T(8,128)} custom-call(bf16[48,48,128]{2,1,0:T(8,128)(2,1)} %bitcast.17, bf16[48,48,128]{2,1,0:T(8,128)(2,1)} %bitcast.18, bf16[48,48,128]{2,1,0:T(8,128)(2,1)} %bitcast.15, f32[48,128]{1,0:T(8,128)} %bitcast.19, f32[48,128]{1,0:T(8,128)} %bitcast.20), custom_call_target="tpu_custom_call" | custom-call | tf_op jit(solution)/shard_map/pallas_call | solution.py:415
  4.5 7.1 %all-to-all-start = ((f32[32,152,128]{2,1,0:T(8,128)}), f32[32,152,128]{2,1,0:T(8,128)S(1)}, u32[]{:S(2)}, u32[]{:S(2)}) async-start(f32[32,152,128]{2,1,0:T(8,128)} %shard_map.68), calls=%async_computation | async-start | bytes 4980736 | tf_op jit(solution)/shard_map/all_to_all | solution.py:433
  11.6 4.1 %shard_map.70 = (f32[144,128]{1,0:T(8,128)S(1)}, f32[144,128]{1,0:T(8,128)S(1)}, f32[144,128]{1,0:T(8,128)S(1)}, f32[144,128]{1,0:T(8,128)S(1)}, f32[144,128]{1,...) custom-call(bf16[48,48,128]{2,1,0:T(8,128)(2,1)} %bitcast.16), custom_call_target="tpu_custom_call" | custom-call | tf_op jit(solution)/shard_map/pallas_call | solution.py:435
  15.7 0.3 collective-permute-start
  16.0 1.5 %collective-permute-start.1 = (f32[144,128]{1,0:T(8,128)S(1)}, f32[144,128]{1,0:T(8,128)S(1)}, u32[]{:S(2)}, u32[]{:S(2)}) collective-permute-start(f32[144,128]{1,0:T(8,128)S(1)} %get-tuple-element.34), channel_id=1, source_target_pairs={{0,2},{1,3},{2,0},{3,1},{4,6},{5,7},{6,4},{7,5},{8,10},{9,11},{10,... | collective-permute-start | bytes 221192 | tf_op jit(solution)/shard_map/ppermute | solution.py:445
  17.5 0.4 collective-permute-start.2
  17.9 1.4 %collective-permute-start.3 = (f32[144,128]{1,0:T(8,128)S(1)}, f32[144,128]{1,0:T(8,128)S(1)}, u32[]{:S(2)}, u32[]{:S(2)}) collective-permute-start(f32[144,128]{1,0:T(8,128)S(1)} %get-tuple-element.36), channel_id=1, source_target_pairs={{0,4},{1,5},{2,6},{3,7},{4,0},{5,1},{6,2},{7,3},{8,12},{9,13},{10,... | collective-permute-start | bytes 221192 | tf_op jit(solution)/shard_map/ppermute | solution.py:445
  19.3 0.3 collective-permute-start.4
  19.6 0.0 collective-permute-done.refs_1_
  19.6 2.3 %collective-permute-start.5 = (f32[144,128]{1,0:T(8,128)S(1)}, f32[144,128]{1,0:T(8,128)S(1)}, u32[]{:S(2)}, u32[]{:S(2)}) collective-permute-start(f32[144,128]{1,0:T(8,128)S(1)} %get-tuple-element.38), channel_id=1, source_target_pairs={{0,6},{1,7},{2,4},{3,5},{4,2},{5,3},{6,0},{7,1},{8,14},{9,15},{10,... | collective-permute-start | bytes 221192 | tf_op jit(solution)/shard_map/ppermute | solution.py:445
  21.9 7.6 %collective-permute-done.1.refs_2_ = f32[144,128]{1,0:T(8,128)S(1)} collective-permute-done((f32[144,128]{1,0:T(8,128)S(1)}, f32[144,128]{1,0:T(8,128)S(1)}, u32[]{:S(2)}, u32[]{:S(2)}) %collective-permute-start.1) | collective-permute-done | bytes 73760 | tf_op jit(solution)/shard_map/ppermute | solution.py:445
  29.5 1.9 %collective-permute-start.6 = (f32[144,128]{1,0:T(8,128)S(1)}, f32[144,128]{1,0:T(8,128)S(1)}, u32[]{:S(2)}, u32[]{:S(2)}) collective-permute-start(f32[144,128]{1,0:T(8,128)S(1)} %get-tuple-element.39), channel_id=1, source_target_pairs={{0,7},{1,6},{2,5},{3,4},{4,3},{5,2},{6,1},{7,0},{8,15},{9,14},{10,... | collective-permute-start | bytes 221192 | tf_op jit(solution)/shard_map/ppermute | solution.py:445
  31.5 2.6 %collective-permute-done.2.refs_3_ = f32[144,128]{1,0:T(8,128)S(1)} collective-permute-done((f32[144,128]{1,0:T(8,128)S(1)}, f32[144,128]{1,0:T(8,128)S(1)}, u32[]{:S(2)}, u32[]{:S(2)}) %collective-permute-start.2) | collective-permute-done | bytes 73760 | tf_op jit(solution)/shard_map/ppermute | solution.py:445
  34.1 0.0 collective-permute-start.7
  34.1 0.0 collective-permute-done.3.refs_0_
  34.1 6.3 %collective-permute-start.8 = (f32[144,128]{1,0:T(8,128)S(1)}, f32[144,128]{1,0:T(8,128)S(1)}, u32[]{:S(2)}, u32[]{:S(2)}) collective-permute-start(f32[144,128]{1,0:T(8,128)S(1)} %get-tuple-element.41), channel_id=1, source_target_pairs={{0,9},{1,8},{2,11},{3,10},{4,13},{5,12},{6,15},{7,14},{8,1},{9,0},... | collective-permute-start | bytes 221192 | tf_op jit(solution)/shard_map/ppermute | solution.py:445
  40.4 0.0 collective-permute-done.4.refs_1_
  40.4 1.5 %collective-permute-start.9 = (f32[144,128]{1,0:T(8,128)S(1)}, f32[144,128]{1,0:T(8,128)S(1)}, u32[]{:S(2)}, u32[]{:S(2)}) collective-permute-start(f32[144,128]{1,0:T(8,128)S(1)} %get-tuple-element.42), channel_id=1, source_target_pairs={{0,10},{1,11},{2,8},{3,9},{4,14},{5,15},{6,12},{7,13},{8,2},{9,3},... | collective-permute-start | bytes 221192 | tf_op jit(solution)/shard_map/ppermute | solution.py:445
  41.8 0.0 collective-permute-done.5.refs_2_
  41.8 0.3 collective-permute-start.10
  42.1 1.3 %collective-permute-done.6.refs_3_ = f32[144,128]{1,0:T(8,128)S(1)} collective-permute-done((f32[144,128]{1,0:T(8,128)S(1)}, f32[144,128]{1,0:T(8,128)S(1)}, u32[]{:S(2)}, u32[]{:S(2)}) %collective-permute-start.6) | collective-permute-done | bytes 73760 | tf_op jit(solution)/shard_map/ppermute | solution.py:445
  43.4 1.4 %collective-permute-start.11 = (f32[144,128]{1,0:T(8,128)}, f32[144,128]{1,0:T(8,128)S(1)}, u32[]{:S(2)}, u32[]{:S(2)}) collective-permute-start(f32[144,128]{1,0:T(8,128)} %get-tuple-element.44), channel_id=1, source_target_pairs={{0,12},{1,13},{2,14},{3,15},{4,8},{5,9},{6,10},{7,11},{8,4},{9,5},... | collective-permute-start | bytes 221192 | tf_op jit(solution)/shard_map/ppermute | solution.py:445
  44.9 9.7 %collective-permute-done.7.refs_0_ = f32[144,128]{1,0:T(8,128)S(1)} collective-permute-done((f32[144,128]{1,0:T(8,128)S(1)}, f32[144,128]{1,0:T(8,128)S(1)}, u32[]{:S(2)}, u32[]{:S(2)}) %collective-permute-start.7) | collective-permute-done | bytes 73760 | tf_op jit(solution)/shard_map/ppermute | solution.py:445
  54.6 4.0 %collective-permute-start.12 = (f32[144,128]{1,0:T(8,128)}, f32[144,128]{1,0:T(8,128)S(1)}, u32[]{:S(2)}, u32[]{:S(2)}) collective-permute-start(f32[144,128]{1,0:T(8,128)} %get-tuple-element.45), channel_id=1, source_target_pairs={{0,13},{1,12},{2,15},{3,14},{4,9},{5,8},{6,11},{7,10},{8,5},{9,4},... | collective-permute-start | bytes 221192 | tf_op jit(solution)/shard_map/ppermute | solution.py:445
  58.6 0.0 collective-permute-done.8.refs_1_
  58.6 1.2 %collective-permute-start.13 = (f32[144,128]{1,0:T(8,128)}, f32[144,128]{1,0:T(8,128)}, u32[]{:S(2)}, u32[]{:S(2)}) collective-permute-start(f32[144,128]{1,0:T(8,128)} %get-tuple-element.46), channel_id=1, source_target_pairs={{0,14},{1,15},{2,12},{3,13},{4,10},{5,11},{6,8},{7,9},{8,6},{9,7},... | collective-permute-start | bytes 221192 | tf_op jit(solution)/shard_map/ppermute | solution.py:445
  59.9 0.0 collective-permute-done.9.refs_2_
  59.9 3.0 %collective-permute-start.14 = (f32[144,128]{1,0:T(8,128)}, f32[144,128]{1,0:T(8,128)}, u32[]{:S(2)}, u32[]{:S(2)}) collective-permute-start(f32[144,128]{1,0:T(8,128)} %get-tuple-element.47), channel_id=1, source_target_pairs={{0,15},{1,14},{2,13},{3,12},{4,11},{5,10},{6,9},{7,8},{8,7},{9,6},... | collective-permute-start | bytes 221192 | tf_op jit(solution)/shard_map/ppermute | solution.py:445
  62.9 5.4 %all-to-all-done.slots_ref = f32[32,152,128]{2,1,0:T(8,128)S(1)} async-done(((f32[32,152,128]{2,1,0:T(8,128)}), f32[32,152,128]{2,1,0:T(8,128)S(1)}, u32[]{:S(2)}, u32[]{:S(2)}) %all-to-all-start) | async-done | bytes 2490400 | tf_op jit(solution)/shard_map/all_to_all | solution.py:433
  68.3 2.8 %shard_map.69 = (f32[3,8,128]{2,1,0:T(8,128)S(1)}, f32[3,8,128]{2,1,0:T(8,128)S(1)}, f32[8,288,128]{2,1,0:T(8,128)S(1)}, f32[8,288,128]{2,1,0:T(8,128)S(1)}, f32...) custom-call(f32[32,152,128]{2,1,0:T(8,128)S(1)} %all-to-all-done.slots_ref), custom_call_target="tpu_custom_call" | custom-call | tf_op jit(solution)/shard_map/pallas_call | solution.py:450
  71.1 0.0 collective-permute-done.10.refs_3_
  71.1 0.4 collective-permute-start.15
  71.5 0.1 shard_map.71.refs_0_
  71.7 0.1 shard_map.72.refs_1_
  71.8 0.1 shard_map.73.refs_2_
  72.0 0.0 collective-permute-done.11.refs_0_
  72.0 0.0 collective-permute-done.12.refs_1_
  72.0 0.0 collective-permute-done.13.refs_2_
  72.0 0.0 collective-permute-done.14.refs_3_
  72.0 1.1 %shard_map.74.refs_3_ = f32[2,288,128]{2,1,0:T(8,128)S(1)} custom-call(f32[144,128]{1,0:T(8,128)S(1)} %collective-permute-done.11.refs_0_, f32[144,128]{1,0:T(8,128)S(1)} %collective-permute-done.12.refs_1_, f32[144,128]{1,0:T(8,128)} %collective-permute-done.13.refs_2_, f32[144,128]{1,0:T(8,128)} %collective-permute-done.14.refs_3_), custom_call_target="tpu_custom_call" | custom-call | tf_op jit(solution)/shard_map/pallas_call | solution.py:447
  73.1 1.5 %collective-permute-done.15.vector_ref = f32[3,8,128]{2,1,0:T(8,128)S(1)} collective-permute-done((f32[3,8,128]{2,1,0:T(8,128)S(1)}, f32[3,8,128]{2,1,0:T(8,128)S(1)}, u32[]{:S(2)}, u32[]{:S(2)}) %collective-permute-start.15) | collective-permute-done | bytes 12320 | tf_op jit(solution)/shard_map/ppermute | solution.py:455
  74.7 0.1 shard_map.76
  74.8 0.6 collective-permute-start.16
  75.4 0.1 shard_map.75.own_ref
  75.5 2.8 %collective-permute-done.16.other_ref = f32[3,8,128]{2,1,0:T(8,128)S(1)} collective-permute-done((f32[3,8,128]{2,1,0:T(8,128)S(1)}, f32[3,8,128]{2,1,0:T(8,128)S(1)}, u32[]{:S(2)}, u32[]{:S(2)}) %collective-permute-start.16) | collective-permute-done | bytes 12320 | tf_op jit(solution)/shard_map/ppermute | solution.py:455
  78.3 2.8 %shard_map.77 = f32[128,128]{1,0:T(8,128)S(1)} custom-call(f32[3,8,128]{2,1,0:T(8,128)S(1)} %shard_map.75.own_ref, f32[3,8,128]{2,1,0:T(8,128)S(1)} %collective-permute-done.16.other_ref, f32[8,288,128]{2,1,0:T(8,128)S(1)} %get-tuple-element.49.forward_ref, f32[8,288,128]{2,1,0:T(8,128)S(1)} %get-tuple-element.50.backward_ref, ...), custom_call_target="tpu_custom_call" | custom-call | tf_op jit(solution)/shard_map/pallas_call | solution.py:461
  81.1 14.2 %all_to_all.10 = f32[32,4,128]{2,1,0:T(4,128)S(1)} all-to-all(f32[32,4,128]{2,1,0:T(4,128)S(1)} %bitcast.13), channel_id=1, replica_groups={{24,16,8,0,25,17,9,1,26,18,10,2,27,19,11,3,28,20,12,4,29,21,13,5,30,22,..., dimensions={0} | all-to-all | bytes 131072 | tf_op jit(solution)/shard_map/all_to_all | solution.py:402
  95.3 1.0 %shard_map.78 = (f32[48,128]{1,0:T(8,128)}, f32[48,128]{1,0:T(8,128)}) custom-call(f32[128,128]{1,0:T(8,128)S(1)} %bitcast.14), custom_call_target="tpu_custom_call" | custom-call | tf_op jit(solution)/shard_map/pallas_call | solution.py:465
Async XLA Ops:
  4.5 63.8 %all-to-all-start = ((f32[32,152,128]{2,1,0:T(8,128)}), f32[32,152,128]{2,1,0:T(8,128)S(1)}, u32[]{:S(2)}, u32[]{:S(2)}) async-start(f32[32,152,128]{2,1,0:T(8,128)} %shard_map.68), calls=%async_computation | async-start | bytes 4980736 | tf_op jit(solution)/shard_map/all_to_all | solution.py:433
  15.7 3.9 %collective-permute-start = (f32[144,128]{1,0:T(8,128)S(1)}, f32[144,128]{1,0:T(8,128)S(1)}, u32[]{:S(2)}, u32[]{:S(2)}) collective-permute-start(f32[144,128]{1,0:T(8,128)S(1)} %get-tuple-element.33), channel_id=1, source_target_pairs={{0,1},{1,0},{2,3},{3,2},{4,5},{5,4},{6,7},{7,6},{8,9},{9,8},{10,11... | collective-permute-start | bytes 221192 | tf_op jit(solution)/shard_map/ppermute | solution.py:445
  16.0 13.5 %collective-permute-start.1 = (f32[144,128]{1,0:T(8,128)S(1)}, f32[144,128]{1,0:T(8,128)S(1)}, u32[]{:S(2)}, u32[]{:S(2)}) collective-permute-start(f32[144,128]{1,0:T(8,128)S(1)} %get-tuple-element.34), channel_id=1, source_target_pairs={{0,2},{1,3},{2,0},{3,1},{4,6},{5,7},{6,4},{7,5},{8,10},{9,11},{10,... | collective-permute-start | bytes 221192 | tf_op jit(solution)/shard_map/ppermute | solution.py:445
  17.5 16.5 %collective-permute-start.2 = (f32[144,128]{1,0:T(8,128)S(1)}, f32[144,128]{1,0:T(8,128)S(1)}, u32[]{:S(2)}, u32[]{:S(2)}) collective-permute-start(f32[144,128]{1,0:T(8,128)S(1)} %get-tuple-element.35), channel_id=1, source_target_pairs={{0,3},{1,2},{2,1},{3,0},{4,7},{5,6},{6,5},{7,4},{8,11},{9,10},{10,... | collective-permute-start | bytes 221192 | tf_op jit(solution)/shard_map/ppermute | solution.py:445
  17.9 16.1 %collective-permute-start.3 = (f32[144,128]{1,0:T(8,128)S(1)}, f32[144,128]{1,0:T(8,128)S(1)}, u32[]{:S(2)}, u32[]{:S(2)}) collective-permute-start(f32[144,128]{1,0:T(8,128)S(1)} %get-tuple-element.36), channel_id=1, source_target_pairs={{0,4},{1,5},{2,6},{3,7},{4,0},{5,1},{6,2},{7,3},{8,12},{9,13},{10,... | collective-permute-start | bytes 221192 | tf_op jit(solution)/shard_map/ppermute | solution.py:445
  19.3 21.0 %collective-permute-start.4 = (f32[144,128]{1,0:T(8,128)S(1)}, f32[144,128]{1,0:T(8,128)S(1)}, u32[]{:S(2)}, u32[]{:S(2)}) collective-permute-start(f32[144,128]{1,0:T(8,128)S(1)} %get-tuple-element.37), channel_id=1, source_target_pairs={{0,5},{1,4},{2,7},{3,6},{4,1},{5,0},{6,3},{7,2},{8,13},{9,12},{10,... | collective-permute-start | bytes 221192 | tf_op jit(solution)/shard_map/ppermute | solution.py:445
  19.6 22.2 %collective-permute-start.5 = (f32[144,128]{1,0:T(8,128)S(1)}, f32[144,128]{1,0:T(8,128)S(1)}, u32[]{:S(2)}, u32[]{:S(2)}) collective-permute-start(f32[144,128]{1,0:T(8,128)S(1)} %get-tuple-element.38), channel_id=1, source_target_pairs={{0,6},{1,7},{2,4},{3,5},{4,2},{5,3},{6,0},{7,1},{8,14},{9,15},{10,... | collective-permute-start | bytes 221192 | tf_op jit(solution)/shard_map/ppermute | solution.py:445
  29.5 13.9 %collective-permute-start.6 = (f32[144,128]{1,0:T(8,128)S(1)}, f32[144,128]{1,0:T(8,128)S(1)}, u32[]{:S(2)}, u32[]{:S(2)}) collective-permute-start(f32[144,128]{1,0:T(8,128)S(1)} %get-tuple-element.39), channel_id=1, source_target_pairs={{0,7},{1,6},{2,5},{3,4},{4,3},{5,2},{6,1},{7,0},{8,15},{9,14},{10,... | collective-permute-start | bytes 221192 | tf_op jit(solution)/shard_map/ppermute | solution.py:445
  34.1 20.5 %collective-permute-start.7 = (f32[144,128]{1,0:T(8,128)S(1)}, f32[144,128]{1,0:T(8,128)S(1)}, u32[]{:S(2)}, u32[]{:S(2)}) collective-permute-start(f32[144,128]{1,0:T(8,128)S(1)} %get-tuple-element.40), channel_id=1, source_target_pairs={{0,8},{1,9},{2,10},{3,11},{4,12},{5,13},{6,14},{7,15},{8,0},{9,1},... | collective-permute-start | bytes 221192 | tf_op jit(solution)/shard_map/ppermute | solution.py:445
  34.1 24.6 %collective-permute-start.8 = (f32[144,128]{1,0:T(8,128)S(1)}, f32[144,128]{1,0:T(8,128)S(1)}, u32[]{:S(2)}, u32[]{:S(2)}) collective-permute-start(f32[144,128]{1,0:T(8,128)S(1)} %get-tuple-element.41), channel_id=1, source_target_pairs={{0,9},{1,8},{2,11},{3,10},{4,13},{5,12},{6,15},{7,14},{8,1},{9,0},... | collective-permute-start | bytes 221192 | tf_op jit(solution)/shard_map/ppermute | solution.py:445
  40.4 19.5 %collective-permute-start.9 = (f32[144,128]{1,0:T(8,128)S(1)}, f32[144,128]{1,0:T(8,128)S(1)}, u32[]{:S(2)}, u32[]{:S(2)}) collective-permute-start(f32[144,128]{1,0:T(8,128)S(1)} %get-tuple-element.42), channel_id=1, source_target_pairs={{0,10},{1,11},{2,8},{3,9},{4,14},{5,15},{6,12},{7,13},{8,2},{9,3},... | collective-permute-start | bytes 221192 | tf_op jit(solution)/shard_map/ppermute | solution.py:445
  41.8 29.3 %collective-permute-start.10 = (f32[144,128]{1,0:T(8,128)}, f32[144,128]{1,0:T(8,128)S(1)}, u32[]{:S(2)}, u32[]{:S(2)}) collective-permute-start(f32[144,128]{1,0:T(8,128)} %get-tuple-element.43), channel_id=1, source_target_pairs={{0,11},{1,10},{2,9},{3,8},{4,15},{5,14},{6,13},{7,12},{8,3},{9,2},... | collective-permute-start | bytes 221192 | tf_op jit(solution)/shard_map/ppermute | solution.py:445
  43.4 28.6 %collective-permute-start.11 = (f32[144,128]{1,0:T(8,128)}, f32[144,128]{1,0:T(8,128)S(1)}, u32[]{:S(2)}, u32[]{:S(2)}) collective-permute-start(f32[144,128]{1,0:T(8,128)} %get-tuple-element.44), channel_id=1, source_target_pairs={{0,12},{1,13},{2,14},{3,15},{4,8},{5,9},{6,10},{7,11},{8,4},{9,5},... | collective-permute-start | bytes 221192 | tf_op jit(solution)/shard_map/ppermute | solution.py:445
  54.6 17.4 %collective-permute-start.12 = (f32[144,128]{1,0:T(8,128)}, f32[144,128]{1,0:T(8,128)S(1)}, u32[]{:S(2)}, u32[]{:S(2)}) collective-permute-start(f32[144,128]{1,0:T(8,128)} %get-tuple-element.45), channel_id=1, source_target_pairs={{0,13},{1,12},{2,15},{3,14},{4,9},{5,8},{6,11},{7,10},{8,5},{9,4},... | collective-permute-start | bytes 221192 | tf_op jit(solution)/shard_map/ppermute | solution.py:445
  58.6 13.4 %collective-permute-start.13 = (f32[144,128]{1,0:T(8,128)}, f32[144,128]{1,0:T(8,128)}, u32[]{:S(2)}, u32[]{:S(2)}) collective-permute-start(f32[144,128]{1,0:T(8,128)} %get-tuple-element.46), channel_id=1, source_target_pairs={{0,14},{1,15},{2,12},{3,13},{4,10},{5,11},{6,8},{7,9},{8,6},{9,7},... | collective-permute-start | bytes 221192 | tf_op jit(solution)/shard_map/ppermute | solution.py:445
  59.9 12.2 %collective-permute-start.14 = (f32[144,128]{1,0:T(8,128)}, f32[144,128]{1,0:T(8,128)}, u32[]{:S(2)}, u32[]{:S(2)}) collective-permute-start(f32[144,128]{1,0:T(8,128)} %get-tuple-element.47), channel_id=1, source_target_pairs={{0,15},{1,14},{2,13},{3,12},{4,11},{5,10},{6,9},{7,8},{8,7},{9,6},... | collective-permute-start | bytes 221192 | tf_op jit(solution)/shard_map/ppermute | solution.py:445
  71.1 3.5 %collective-permute-start.15 = (f32[3,8,128]{2,1,0:T(8,128)S(1)}, f32[3,8,128]{2,1,0:T(8,128)S(1)}, u32[]{:S(2)}, u32[]{:S(2)}) collective-permute-start(f32[3,8,128]{2,1,0:T(8,128)S(1)} %get-tuple-element.48), channel_id=1, source_target_pairs={{0,16},{1,17},{2,18},{3,19},{4,20},{5,21},{6,22},{7,23},{8,24},{9,... | collective-permute-start | bytes 36872 | tf_op jit(solution)/shard_map/ppermute | solution.py:455
  74.8 3.5 %collective-permute-start.16 = (f32[3,8,128]{2,1,0:T(8,128)S(1)}, f32[3,8,128]{2,1,0:T(8,128)S(1)}, u32[]{:S(2)}, u32[]{:S(2)}) collective-permute-start(f32[3,8,128]{2,1,0:T(8,128)S(1)} %shard_map.76), channel_id=1, source_target_pairs={{0,16},{1,17},{2,18},{3,19},{4,20},{5,21},{6,22},{7,23},{8,24},{9,... | collective-permute-start | bytes 36872 | tf_op jit(solution)/shard_map/ppermute | solution.py:455
